TPU v7x, 32 devices: a whole 2x2x4 slice. The times are simulated.
32 devices in a mesh: grp: 2 (over x), tile: 8 (over z, y), pos: 2 (over core).
Axes of the slice: x: 2, y: 2, z: 4, core: 2. Of those that a mesh axis runs over, the one named last changes fastest.
Arguments:
- object_slices: bfloat16 [2, 4, 2048, 512], P('pos', 'grp', 'tile'), parts along dimension 1, may hold values from -6 to 6
- probe: bfloat16 [4, 256, 256], P('grp'), parts along dimension 0, may hold values from -4 to 4
- intensity: bfloat16 [8, 16, 2, 256, 256], P('tile', 'grp', 'pos'), parts along dimension 1, may hold values from 0.099609375 to 2
- scan_rows: int32 [8, 16, 2], P('tile', 'grp', 'pos'), parts along dimension 1, may hold values from 0 to 255, as said below
- scan_cols: int32 [8, 16, 2], P('tile', 'grp', 'pos'), parts along dimension 1, may hold values from 0 to 256
- counts: int32 [2, 8], P('grp', 'tile'), parts along dimension 0, may hold values from 1 to 16, as said below
Outputs:
- object_grad: float32 [2, 4, 2048, 512], P('pos', 'grp', 'tile'), parts along dimension 1
- probe_grad: float32 [4, 256, 256], P('grp'), parts along dimension 0
There are 2 independent parts, one for each index of `grp`. A program takes and returns all parts, laid end to end along the dimension named above; each array names one. Nothing has to cross between parts.
Inputs may be any that keep to these rules, and one draw needn't show every extreme that they name: `scan_rows`: offsets of the last strip's positions are at most 0, so every window lies inside the object. `counts`: slots whose position is not live hold arbitrary values, which must be ignored; some strip is full and some strip has one live position.
All inputs are finite; a program needn't handle non-finite values.
Results may differ from a plain program's by a relative error of at most 0.0098.
Values may be sent and summed in bfloat16 or wider, within the bound.
No kernel may reach another device: no remote copies, remote signals or barrier semaphores. Data moves between devices by JAX's collectives and lax.ppermute only.
A program may use at most 64 MiB of HBM per device.

v0:
```python
import math

import jax
import jax.numpy as jnp
from jax import lax
from jax.sharding import PartitionSpec as P

BAND = 32


def from_behind(value, axis, by):
    peers = lax.axis_size(axis)
    pairs = [(i, i + by) for i in range(peers) if 0 <= i + by < peers]
    return lax.ppermute(value, axis, pairs)


def make_tables(size, band):
    index = jnp.arange(size, dtype=jnp.int32)
    offset = index[:, None] - index[None, :]
    inside = (jnp.abs(offset) <= band).astype(jnp.float32)
    offset_f = offset.astype(jnp.float32)
    phase = math.pi * offset_f * offset_f / (2.0 * band)
    scale = 1.0 / math.sqrt(2 * band + 1)
    prop_re = (jnp.cos(phase) * inside * scale).astype(jnp.bfloat16)
    prop_im = (jnp.sin(phase) * inside * scale).astype(jnp.bfloat16)
    product = index[:, None] * index[None, :] % size
    angle = -2.0 * math.pi * product.astype(jnp.float32) / size
    four_re = (jnp.cos(angle) / math.sqrt(size)).astype(jnp.bfloat16)
    four_im = (jnp.sin(angle) / math.sqrt(size)).astype(jnp.bfloat16)
    return (prop_re, prop_im, -prop_im, four_re, four_im, -four_im)


def matdot(left, right):
    return jnp.dot(left, right, preferred_element_type=jnp.float32)


def left_mul(mat_re, mat_im, val_re, val_im):
    return (
        matdot(mat_re, val_re) - matdot(mat_im, val_im),
        matdot(mat_re, val_im) + matdot(mat_im, val_re),
    )


def right_mul(val_re, val_im, mat_re, mat_im):
    return (
        matdot(val_re, mat_re) - matdot(val_im, mat_im),
        matdot(val_re, mat_im) + matdot(val_im, mat_re),
    )


def to_half(value):
    return value.astype(jnp.bfloat16)


def position_terms(window, probe, measured, table_set):
    prop_re, prop_im, prop_neg, four_re, four_im, four_neg = table_set
    first_re = window[0, 0].astype(jnp.float32)
    first_im = window[0, 1].astype(jnp.float32)
    second_re = window[1, 0].astype(jnp.float32)
    second_im = window[1, 1].astype(jnp.float32)
    probe_re = probe[0].astype(jnp.float32)
    probe_im = probe[1].astype(jnp.float32)
    enter_re = to_half(probe_re * first_re - probe_im * first_im)
    enter_im = to_half(probe_re * first_im + probe_im * first_re)
    half_re, half_im = left_mul(prop_re, prop_im, enter_re, enter_im)
    after_re, after_im = right_mul(to_half(half_re), to_half(half_im), prop_re, prop_im)
    exit_re = to_half(after_re * second_re - after_im * second_im)
    exit_im = to_half(after_re * second_im + after_im * second_re)
    far_re, far_im = left_mul(four_re, four_im, exit_re, exit_im)
    wave_re, wave_im = right_mul(to_half(far_re), to_half(far_im), four_re, four_im)
    misfit = wave_re * wave_re + wave_im * wave_im - measured.astype(jnp.float32)
    back_re = to_half(misfit * wave_re)
    back_im = to_half(misfit * wave_im)
    near_re, near_im = left_mul(four_re, four_neg, back_re, back_im)
    exit_gre, exit_gim = right_mul(to_half(near_re), to_half(near_im), four_re, four_neg)
    grad_second = jnp.stack(
        [exit_gre * after_re + exit_gim * after_im, exit_gim * after_re - exit_gre * after_im]
    )
    mid_re = to_half(exit_gre * second_re + exit_gim * second_im)
    mid_im = to_half(exit_gim * second_re - exit_gre * second_im)
    prev_re, prev_im = left_mul(prop_re, prop_neg, mid_re, mid_im)
    enter_gre, enter_gim = right_mul(to_half(prev_re), to_half(prev_im), prop_re, prop_neg)
    grad_first = jnp.stack(
        [enter_gre * probe_re + enter_gim * probe_im, enter_gim * probe_re - enter_gre * probe_im]
    )
    probe_term = jnp.stack(
        [enter_gre * first_re + enter_gim * first_im, enter_gim * first_re - enter_gre * first_im]
    )
    return (jnp.stack([grad_first, grad_second]), probe_term)


def local(object_slices, probe, intensity, scan_rows, scan_cols, counts):
    strip_rows = object_slices.shape[2]
    probe_size = probe.shape[1]
    slot_count = intensity.shape[1]
    table_set = make_tables(probe_size, BAND)
    both_slices = lax.all_gather(object_slices, "pos", axis=0, tiled=True)
    below = from_behind(both_slices, "tile", -1)
    extended = jnp.concatenate([both_slices, below], axis=2)
    slice_count = extended.shape[0]
    cores = lax.axis_size("pos")
    my_core = lax.axis_index("pos")
    live_slots = jnp.minimum(
        jnp.maximum(counts[0, 0] - my_core + cores - 1, 0) // cores, slot_count
    )
    zero = jnp.zeros((), jnp.int32)
    block = (slice_count, 2, probe_size, probe_size)

    def visit(slot, carry):
        grad_ext, grad_probe = carry
        starts = (zero, zero, scan_rows[0, slot, 0], scan_cols[0, slot, 0])
        window = lax.dynamic_slice(extended, starts, block)
        grad_win, probe_term = position_terms(window, probe, intensity[0, slot, 0], table_set)
        previous = lax.dynamic_slice(grad_ext, starts, block)
        grad_ext = lax.dynamic_update_slice(grad_ext, previous + grad_win, starts)
        return (grad_ext, grad_probe + probe_term)

    start = (jnp.zeros(extended.shape, jnp.float32), jnp.zeros(probe.shape, jnp.float32))
    grad_ext, grad_probe = lax.fori_loop(0, live_slots, visit, start)
    from_above = from_behind(grad_ext[:, :, strip_rows:, :].astype(jnp.bfloat16), "tile", 1).astype(
        jnp.float32
    )
    strip_grad = grad_ext[:, :, :strip_rows, :] + from_above
    summed = lax.psum(strip_grad.astype(jnp.bfloat16), "pos").astype(jnp.float32)
    owned = lax.dynamic_slice_in_dim(summed, my_core, 1, 0)
    total_slots = lax.axis_size("tile") * slot_count * cores
    probe_total = lax.psum(grad_probe, ("tile", "pos"))
    return (owned, probe_total / math.sqrt(total_slots))


def solution(mesh):
    placed = (
        P("pos", "grp", "tile", None),
        P("grp", None, None),
        P("tile", "grp", "pos", None, None),
        P("tile", "grp", "pos"),
        P("tile", "grp", "pos"),
        P("grp", "tile"),
    )
    return jax.shard_map(
        local,
        mesh=mesh,
        in_specs=placed,
        out_specs=(P("pos", "grp", "tile", None), P("grp", None, None)),
        check_vma=False,
    )
```

profile of v0, /device:TPU:16, one launch (start us, length us, event | category | flops | bytes accessed | tf_op | source)
XLA Modules:
  0.0 617.4 jit_solution(15706300624155771952)
XLA Ops:
  7.9 12.0 %all-gather.2.cloned.1.call-done = bf16[2,2,256,512]{3,2,1,0:T(8,128)(2,1)} async-done(((bf16[1,2,256,512]{3,2,1,0:T(8,128)(2,1)}), bf16[2,2,256,512]{3,2,1,0:T(8,128)(2,1)}) %all-gather.2.cloned.1.call-update) | async-done | bytes 1048592 | tf_op jit(solution)/shard_map/all_gather | solution.py:97
  19.9 3.3 collective-permute-start
  24.0 23.4 %collective-permute-done = bf16[2,2,256,512]{3,2,1,0:T(8,128)(2,1)S(1)} collective-permute-done((bf16[2,2,256,512]{3,2,1,0:T(8,128)(2,1)}, bf16[2,2,256,512]{3,2,1,0:T(8,128)(2,1)S(1)}, u32[]{:S(2)}, u32[]{:S(2)}) %collective-permute-start) | collective-permute-done | bytes 1048608 | tf_op jit(solution)/shard_map/ppermute | solution.py:14
  47.4 2.7 pad_maximum_fusion
  50.2 2.5 broadcast_in_dim.4
  52.7 108.0 %while.14 = (s32[]{:T(128)}, f32[2,2,512,512]{3,2,1,0:T(8,128)}, f32[2,256,256]{2,1,0:T(8,128)S(1)}, s32[]{:T(128)}, s32[1,8,1]{1,2,0:T(1,128)S(1)}, /*index=5*/...) while((s32[]{:T(128)}, f32[2,2,512,512]{3,2,1,0:T(8,128)}, ...), condition=%wide.region_1.2_spmd.clone.clone, body=%wide.region_0.1_spmd.clone.clone.sunk | while | flops 1109327872 | bytes 29753684 | solution.py:119
  57.0 1.2 fusion.377
  60.5 0.8 fusion.382
  62.0 0.8 fusion.380
  62.8 0.8 convolution_add_fusion.11
  63.6 1.9 fusion.384
  65.5 1.1 fusion.385
  66.6 1.1 fusion.386
  67.7 1.1 fusion.388
  68.9 1.1 fusion.389
  70.0 1.1 fusion.390
  71.2 1.1 fusion.387
  72.3 1.2 convolution_subtract_fusion.9
  73.5 2.1 multiply_convert_fusion.75
  75.6 1.1 fusion.391
  76.7 1.1 fusion.392
  77.9 1.1 fusion.394
  79.0 1.1 fusion.395
  80.2 1.1 fusion.396
  81.3 1.1 fusion.393
  82.5 1.1 convolution_add_fusion.12
  83.6 2.3 fusion.397
  86.7 0.8 fusion.399
  89.8 0.8 fusion.400
  91.4 1.9 fusion.404
  93.4 1.8 maximum_add_fusion.4
  95.3 11.6 %dynamic_update_slice.6 = f32[2,2,512,512]{3,2,1,0:T(8,128)} dynamic-update-slice(f32[2,2,512,512]{3,2,1,0:T(8,128)} %get-tuple-element.401, f32[2,2,256,256]{3,2,1,0:T(8,128)S(1)} %maximum_add_fusion.4, s32[]{:T(128)} %constant.59.clone.1..sunk, s32[]{:T(128)} %constant.59.clone.1..sunk, s32[]{:T(128)S(6)} %select_n.147, s32[]{:T(128)S(6)} %select_n.148) | dynamic-update-slice | bytes 2097156 | tf_op jit(solution)/shard_map/while/body/dynamic_update_slice | solution.py:115
  111.2 1.2 fusion.377
  116.3 0.8 fusion.380
  117.8 1.9 fusion.384
  119.7 1.1 fusion.385
  120.8 1.1 fusion.386
  122.0 1.1 fusion.388
  123.1 1.1 fusion.389
  124.3 1.1 fusion.390
  125.4 1.1 fusion.387
  126.6 1.2 convolution_subtract_fusion.9
  127.7 2.1 multiply_convert_fusion.75
  129.8 1.1 fusion.391
  130.9 1.1 fusion.392
  132.1 1.1 fusion.394
  133.2 1.1 fusion.395
  134.4 1.1 fusion.396
  135.5 1.1 fusion.393
  136.7 1.1 convolution_add_fusion.12
  137.8 2.3 fusion.397
  141.0 0.8 fusion.399
  144.0 0.8 fusion.400
  145.6 1.9 fusion.404
  147.6 1.8 maximum_add_fusion.4
  149.5 11.1 %dynamic_update_slice.6 = f32[2,2,512,512]{3,2,1,0:T(8,128)} dynamic-update-slice(f32[2,2,512,512]{3,2,1,0:T(8,128)} %get-tuple-element.401, f32[2,2,256,256]{3,2,1,0:T(8,128)S(1)} %maximum_add_fusion.4, s32[]{:T(128)} %constant.59.clone.1..sunk, s32[]{:T(128)} %constant.59.clone.1..sunk, s32[]{:T(128)S(6)} %select_n.147, s32[]{:T(128)S(6)} %select_n.148) | dynamic-update-slice | bytes 2097156 | tf_op jit(solution)/shard_map/while/body/dynamic_update_slice | solution.py:115
  160.7 1.9 slice.50
  162.6 114.2 %collective-permute-start.1 = (bf16[2,2,256,512]{3,2,1,0:T(8,128)(2,1)S(1)}, bf16[2,2,256,512]{3,2,1,0:T(8,128)(2,1)S(1)}, u32[]{:S(2)}, u32[]{:S(2)}) collective-permute-start(bf16[2,2,256,512]{3,2,1,0:T(8,128)(2,1)S(1)} %slice.50), channel_id=1, source_target_pairs={{0,2},{2,4},{4,6},{6,8},{8,10},{10,12},{12,14},{1,3},{3,5},{5,7},{... | collective-permute-start | bytes 3145736 | tf_op jit(solution)/shard_map/ppermute | solution.py:14
  276.8 21.8 %collective-permute-done.1 = bf16[2,2,256,512]{3,2,1,0:T(8,128)(2,1)S(1)} collective-permute-done((bf16[2,2,256,512]{3,2,1,0:T(8,128)(2,1)S(1)}, bf16[2,2,256,512]{3,2,1,0:T(8,128)(2,1)S(1)}, u32[]{:S(2)}, u32[]{:S(2)}) %collective-permute-start.1) | collective-permute-done | bytes 1048608 | tf_op jit(solution)/shard_map/ppermute | solution.py:14
  298.6 2.9 add_convert_fusion
  301.6 284.3 %all-reduce.5.cloned.1.call-done = f32[2,256,256]{2,1,0:T(8,128)} async-done(((f32[2,256,256]{2,1,0:T(8,128)}), f32[2,256,256]{2,1,0:T(8,128)}) %all-reduce.5.cloned.1.call-update) | async-done | bytes 524304 | tf_op jit(solution)/shard_map/psum | solution.py:127
  585.9 1.9 broadcast_multiply_fusion
  587.8 20.9 %all-reduce.3.cloned.1.call-done = bf16[2,2,256,512]{3,2,1,0:T(8,128)(2,1)} async-done(((bf16[2,2,256,512]{3,2,1,0:T(8,128)(2,1)}), bf16[2,2,256,512]{3,2,1,0:T(8,128)(2,1)}) %all-reduce.3.cloned.1.call-update) | async-done | bytes 1048592 | tf_op jit(solution)/shard_map/psum | solution.py:124
  608.7 2.1 dynamic-slice_convert_fusion
  (43 shorter events, 17.8 us)
Async XLA Ops:
  7.2 12.8 %all-gather.2.cloned.1.call-start = ((), (), s32[]{:S(2)}) async-start(), calls=%async_computation | async-start | bytes 1572864 | tf_op jit(solution)/shard_map/all_gather | solution.py:97
  7.9 578.0 %all-reduce.5.cloned.1.call-start = ((), (), s32[]{:S(2)}) async-start(), calls=%async_computation.2 | async-start | bytes 1048576 | tf_op jit(solution)/shard_map/psum | solution.py:127
  19.9 27.5 %collective-permute-start = (bf16[2,2,256,512]{3,2,1,0:T(8,128)(2,1)}, bf16[2,2,256,512]{3,2,1,0:T(8,128)(2,1)S(1)}, u32[]{:S(2)}, u32[]{:S(2)}) collective-permute-start(bf16[2,2,256,512]{3,2,1,0:T(8,128)(2,1)} %all-gather.2.cloned.1.call-done), channel_id=1, source_target_pairs={{2,0},{4,2},{6,4},{8,6},{10,8},{12,10},{14,12},{3,1},{5,3},{7,5},{... | collective-permute-start | bytes 3145736 | tf_op jit(solution)/shard_map/ppermute | solution.py:14
  50.2 2.5 copy-start.1
  50.2 2.5 copy-start.2
  50.2 2.5 copy-start.3
  160.7 116.1 %copy-start = (f32[2,256,256]{2,1,0:T(8,128)}, f32[2,256,256]{2,1,0:T(8,128)S(1)}, u32[]{:S(2)}) copy-start(f32[2,256,256]{2,1,0:T(8,128)S(1)} %get-tuple-element.119) | copy-start | bytes 1572868
  162.6 136.1 %collective-permute-start.1 = (bf16[2,2,256,512]{3,2,1,0:T(8,128)(2,1)S(1)}, bf16[2,2,256,512]{3,2,1,0:T(8,128)(2,1)S(1)}, u32[]{:S(2)}, u32[]{:S(2)}) collective-permute-start(bf16[2,2,256,512]{3,2,1,0:T(8,128)(2,1)S(1)} %slice.50), channel_id=1, source_target_pairs={{0,2},{2,4},{4,6},{6,8},{8,10},{10,12},{12,14},{1,3},{3,5},{5,7},{... | collective-permute-start | bytes 3145736 | tf_op jit(solution)/shard_map/ppermute | solution.py:14
  276.8 331.9 %all-reduce.3.cloned.1.call-start = ((), (), s32[]{:S(2)}) async-start(), calls=%async_computation.1 | async-start | bytes 2097152 | tf_op jit(solution)/shard_map/psum | solution.py:124
Sparse Core Ops, SparseCore 0:
  9.5 10.3 all-gather.1
  276.9 308.9 all-reduce.4
  588.8 19.8 all-reduce.2
where the time goes:
time: 622 us; the launch traced here: 617 us
  waiting for transfers between devices  363 us (58%)
  starting transfers between devices  118 us (19%)
  matrix products  69.7 us (11%)
  local copies, waits for them, and re-layouts  28.5 us (5%)
  other arithmetic  16.2 us (3%)
  between operations  14.5 us (2%)
  loops' own time  7.7 us (1%)
    psum x1, waiting for transfers between devices, local(): probe_total = lax.psum(grad_probe, ('tile', 'pos'))  284 us
    ppermute x2, starting transfers between devices, from_behind(): return lax.ppermute(value, axis, pairs)  118 us
    dot_general x64, matrix products, matdot(): return jnp.dot(left, right, preferred_element_type=jnp.float32)  69.7 us
    ppermute x2, waiting for transfers between devices, from_behind(): return lax.ppermute(value, axis, pairs)  45.2 us
    dynamic_update_slice x2, local copies, waits for them, and re-layouts, visit(): grad_ext = lax.dynamic_update_slice(grad_ext, previous + grad_win, starts)  22.8 us
    psum x1, waiting for transfers between devices, local(): lax.psum(strip_grad.astype(jnp.bfloat16), 'pos').astype(jnp.float32)  20.9 us
  transfers between devices with their start and end apart: 5, of which 5 were waited for; matrix products, arithmetic and copies ran while one was open for 1% of the time, Pallas kernels for 0%

commit v1 on v0

v1 whole, which is shorter than its diff:
```python
import math

import jax
import jax.numpy as jnp
import ml_dtypes
import numpy as np
from jax import lax
from jax.experimental import pallas as pl
from jax.experimental.pallas import tpu as pltpu
from jax.sharding import PartitionSpec as P

BAND = 32
LANES = 128
CHUNK = 16
WIN_CHUNK = 32
VMEM_BYTES = 56 * 1024 * 1024
f32 = jnp.float32
bf16 = jnp.bfloat16


def tables(size):
    index = np.arange(size, dtype=np.int32)
    offset = index[:, None] - index[None, :]
    inside = (np.abs(offset) <= BAND).astype(np.float32)
    offset_f = offset.astype(np.float32)
    phase = (np.float32(math.pi) * offset_f * offset_f / np.float32(2.0 * BAND)).astype(np.float32)
    scale = np.float32(1.0 / math.sqrt(2 * BAND + 1))
    prop_re = np.cos(phase) * inside * scale
    prop_im = np.sin(phase) * inside * scale
    product = (index[:, None] * index[None, :]) % size
    angle = (np.float32(-2.0 * math.pi) * product.astype(np.float32) / np.float32(size)).astype(np.float32)
    root = np.float32(math.sqrt(size))
    return prop_re, prop_im, np.cos(angle) / root, np.sin(angle) / root


def packed(mat_re, mat_im):
    n, k = mat_re.shape
    upper = np.concatenate([mat_re, -mat_im], axis=1).reshape(n // CHUNK, 1, CHUNK, 2 * k)
    lower = np.concatenate([mat_im, mat_re], axis=1).reshape(n // CHUNK, 1, CHUNK, 2 * k)
    both = np.concatenate([upper, lower], axis=1).reshape(2 * n, 2 * k)
    return both.astype(np.float32).astype(ml_dtypes.bfloat16)


def constants(size):
    half = size // 2
    kr, ki, fr, fi = tables(size)
    near, far = half + BAND, half - BAND
    prop = [
        packed(kr[:near, :half], ki[:near, :half]),
        packed(kr[far:, half:], ki[far:, half:]),
        packed(kr[:near, :half], -ki[:near, :half]),
        packed(kr[far:, half:], -ki[far:, half:]),
    ]
    four = [
        packed(fr[0::2, :half], fi[0::2, :half]),
        packed(fr[1::2, :half], fi[1::2, :half]),
        packed(fr[:half, 0::2], -fi[:half, 0::2]),
        packed(fr[:half, 1::2], -fi[:half, 1::2]),
    ]
    order = np.concatenate([np.arange(0, size, 2), np.arange(1, size, 2)])
    perm = np.eye(size, dtype=np.float32)[order].astype(ml_dtypes.bfloat16)
    return np.stack(prop), np.stack(four), perm


def nt(left, right):
    return lax.dot_general(left, right, (((1,), (1,)), ((), ())), preferred_element_type=f32)


def kernel(
    rows_ref, cols_ref, info_ref,
    own_ref, other_ref, halo_own_ref, halo_other_ref, probe_ref, meas_ref, prop_ref, four_ref, perm_ref,
    strip_ref, tail_ref, send_ref, probe_out_ref,
    ext, acc, win, wave, x_a, x_b, pro,
):
    size = probe_ref.shape[1]
    half = size // 2
    strip = own_ref.shape[1]
    ny = own_ref.shape[2]
    blocks = ny // LANES
    steps = size // CHUNK
    core = info_ref[0]
    live = info_ref[1]

    for at, source in ((0, own_ref), (1, other_ref)):
        which = core if at == 0 else 1 - core
        lower = halo_own_ref if at == 0 else halo_other_ref
        for part in range(2):
            for block in range(blocks):
                lanes = slice(block * LANES, (block + 1) * LANES)
                ext[which, part, block, :strip, :] = source[part, :, lanes].astype(f32)
                ext[which, part, block, strip:, :] = lower[part, :, lanes].astype(f32)
    acc[...] = jnp.zeros(acc.shape, f32)
    probe_out_ref[...] = jnp.zeros(probe_out_ref.shape, f32)
    pro[...] = probe_ref[...].astype(f32)

    def banded(base, source):
        first = nt(prop_ref[base], source[:, :size])
        second = nt(prop_ref[base + 1], source[:, size:])
        skip = (half - BAND) // CHUNK
        stop = (half + BAND) // CHUNK

        def at(j):
            out = []
            for part in range(2):
                value = None
                if j < stop:
                    lo = (2 * j + part) * CHUNK
                    value = first[lo : lo + CHUNK]
                if j >= skip:
                    lo = (2 * (j - skip) + part) * CHUNK
                    more = second[lo : lo + CHUNK]
                    value = more if value is None else value + more
                out.append(value)
            return out

        return at

    def halves(base, source):
        first = nt(four_ref[base], source[:, :size])
        second = nt(four_ref[base + 1], source[:, size:])

        def at(j):
            lo = 2 * j * CHUNK
            return (
                (first[lo : lo + CHUNK], first[lo + CHUNK : lo + 2 * CHUNK]),
                (second[lo : lo + CHUNK], second[lo + CHUNK : lo + 2 * CHUNK]),
            )

        return at

    def put(target, lo, re, im):
        target[lo : lo + CHUNK, :] = jnp.concatenate(
            [re[:, :half], im[:, :half], re[:, half:], im[:, half:]], axis=1
        ).astype(bf16)

    def put_butterfly(target, lo, re, im):
        target[lo : lo + CHUNK, :] = jnp.concatenate(
            [
                re[:, :half] + re[:, half:],
                im[:, :half] + im[:, half:],
                re[:, :half] - re[:, half:],
                im[:, :half] - im[:, half:],
            ],
            axis=1,
        ).astype(bf16)

    def visit(slot, _):
        row = rows_ref[slot]
        col = cols_ref[slot]
        block_at = lax.shift_right_logical(col, 7)
        shift = jnp.bitwise_and(col, LANES - 1)
        back = jnp.bitwise_and(LANES - shift, LANES - 1)
        keep = lax.broadcasted_iota(jnp.int32, (WIN_CHUNK, LANES), 1) < LANES - shift
        low = lax.broadcasted_iota(jnp.int32, (CHUNK, LANES), 1) < shift

        def scatter(which, lo, parts):
            for part, value in enumerate(parts):
                left = pltpu.roll(value[:, :LANES], shift, 1)
                right = pltpu.roll(value[:, LANES:], shift, 1)
                pieces = (
                    jnp.where(low, 0.0, left),
                    jnp.where(low, left, right),
                    jnp.where(low, right, 0.0),
                )
                for i, piece in enumerate(pieces):
                    at = (which, part, block_at + i, pl.ds(row + lo, CHUNK), slice(None))
                    acc[at] = acc[at] + piece

        for lo in range(0, size, WIN_CHUNK):
            span = slice(lo, lo + WIN_CHUNK)
            for which in range(2):
                for part in range(2):
                    loaded = [
                        pltpu.roll(ext[which, part, block_at + i, pl.ds(row + lo, WIN_CHUNK), :], back, 1)
                        for i in range(3)
                    ]
                    win[which, part, span, :LANES] = jnp.where(keep, loaded[0], loaded[1])
                    win[which, part, span, LANES:] = jnp.where(keep, loaded[1], loaded[2])

        for j in range(steps):
            span = slice(j * CHUNK, (j + 1) * CHUNK)
            pr, pi = pro[0, span], pro[1, span]
            wr, wi = win[0, 0, span], win[0, 1, span]
            put(x_a, j * CHUNK, pr * wr - pi * wi, pr * wi + pi * wr)

        at = banded(0, x_a[...])
        for j in range(steps):
            re, im = at(j)
            put(x_b, j * CHUNK, re, im)

        at = banded(0, x_b[...])
        for j in range(steps):
            span = slice(j * CHUNK, (j + 1) * CHUNK)
            re, im = at(j)
            wave[0, span] = re
            wave[1, span] = im
            wr, wi = win[1, 0, span], win[1, 1, span]
            put_butterfly(x_a, j * CHUNK, re * wr - im * wi, re * wi + im * wr)

        at = halves(0, x_a[...])
        for j in range(steps // 2):
            even, odd = at(j)
            put_butterfly(x_b, j * CHUNK, *even)
            put_butterfly(x_b, half + j * CHUNK, *odd)

        at = halves(0, x_b[...])
        for j in range(steps // 2):
            for side, (re, im) in enumerate(at(j)):
                lo = side * half + j * CHUNK
                misfit = re * re + im * im - meas_ref[slot, lo : lo + CHUNK, :].astype(f32)
                put(x_a, lo, misfit * re, misfit * im)

        at = halves(2, x_a[...])
        for j in range(steps // 2):
            (er, ei), (dr, di) = at(j)
            put(x_b, j * CHUNK, er + dr, ei + di)
            put(x_b, half + j * CHUNK, er - dr, ei - di)

        at = halves(2, x_b[...])
        for j in range(steps // 2):
            (er, ei), (dr, di) = at(j)
            for side in range(2):
                lo = side * half + j * CHUNK
                span = slice(lo, lo + CHUNK)
                re, im = (er + dr, ei + di) if side == 0 else (er - dr, ei - di)
                br, bi = wave[0, span], wave[1, span]
                wr, wi = win[1, 0, span], win[1, 1, span]
                scatter(1, lo, (re * br + im * bi, im * br - re * bi))
                put(x_a, lo, re * wr + im * wi, im * wr - re * wi)

        at = banded(2, x_a[...])
        for j in range(steps):
            re, im = at(j)
            put(x_b, j * CHUNK, re, im)

        at = banded(2, x_b[...])
        for j in range(steps):
            lo = j * CHUNK
            span = slice(lo, lo + CHUNK)
            re, im = at(j)
            pr, pi = pro[0, span], pro[1, span]
            wr, wi = win[0, 0, span], win[0, 1, span]
            scatter(0, lo, (re * pr + im * pi, im * pr - re * pi))
            probe_out_ref[0, span] = probe_out_ref[0, span] + (re * wr + im * wi)
            probe_out_ref[1, span] = probe_out_ref[1, span] + (im * wr - re * wi)
        return 0

    lax.fori_loop(0, live, visit, 0)

    for part in range(2):
        for block in range(blocks):
            lanes = slice(block * LANES, (block + 1) * LANES)
            strip_ref[part, :, lanes] = acc[core, part, block, :strip, :]
            tail_ref[part, :, lanes] = acc[core, part, block, strip:, :]
            send_ref[part, :, lanes] = acc[1 - core, part, block, :, :].astype(bf16)


def swap(value):
    return lax.ppermute(value, "pos", [(0, 1), (1, 0)])


def shift_tile(value, by):
    peers = lax.axis_size("tile")
    return lax.ppermute(value, "tile", [(i, i + by) for i in range(peers) if 0 <= i + by < peers])


def local(object_slices, probe, intensity, scan_rows, scan_cols, counts):
    strip, ny = object_slices.shape[2:]
    size = probe.shape[1]
    slots = intensity.shape[1]
    cores = lax.axis_size("pos")
    core = lax.axis_index("pos")
    prop, four, perm = constants(size)
    own = object_slices[0]
    other = swap(own)
    halo_own = shift_tile(own, -1)
    halo_other = swap(halo_own)
    order = np.concatenate([np.arange(0, size, 2), np.arange(1, size, 2)])
    measured = intensity.reshape(slots, size // 2, 2, size // 2, 2).transpose(0, 2, 1, 4, 3).reshape(slots, size, size)
    live = jnp.minimum(jnp.maximum(counts[0, 0] - core + cores - 1, 0) // cores, slots)
    info = jnp.stack([core, live]).astype(jnp.int32)
    vmem = pl.BlockSpec(memory_space=pltpu.VMEM)
    smem = pl.BlockSpec(memory_space=pltpu.SMEM)
    blocks = ny // LANES + 1
    strip_grad, tail, send, grad_probe = pl.pallas_call(
        kernel,
        out_shape=(
            jax.ShapeDtypeStruct((2, strip, ny), f32),
            jax.ShapeDtypeStruct((2, strip, ny), f32),
            jax.ShapeDtypeStruct((2, 2 * strip, ny), bf16),
            jax.ShapeDtypeStruct((2, size, size), f32),
        ),
        in_specs=[smem] * 3 + [vmem] * 9,
        out_specs=(vmem,) * 4,
        scratch_shapes=[
            pltpu.VMEM((2, 2, blocks, 2 * strip, LANES), f32),
            pltpu.VMEM((2, 2, blocks, 2 * strip, LANES), f32),
            pltpu.VMEM((2, 2, size, size), f32),
            pltpu.VMEM((2, size, size), f32),
            pltpu.VMEM((size, 2 * size), bf16),
            pltpu.VMEM((size, 2 * size), bf16),
            pltpu.VMEM((2, size, size), f32),
        ],
        compiler_params=pltpu.CompilerParams(vmem_limit_bytes=VMEM_BYTES),
    )(
        scan_rows[0, :, 0], scan_cols[0, :, 0], info,
        own, other, halo_own, halo_other, probe, measured,
        jnp.asarray(prop), jnp.asarray(four), jnp.asarray(perm),
    )
    got = swap(send).astype(f32)
    tail_sum = (tail + got[:, strip:]).astype(bf16)
    from_above = shift_tile(tail_sum, 1).astype(f32)
    owned = (strip_grad + got[:, :strip] + from_above)[None]
    total_slots = lax.axis_size("tile") * slots * cores

    mine = lax.dynamic_index_in_dim(grad_probe, core, 0, keepdims=False)
    theirs = lax.dynamic_index_in_dim(grad_probe, 1 - core, 0, keepdims=False)
    part = mine + swap(theirs)
    peers = lax.axis_size("tile")
    step = 1
    while step < peers:
        part = part + lax.ppermute(part, "tile", [(i, i ^ step) for i in range(peers)])
        step *= 2
    part = part / math.sqrt(total_slots)
    again = swap(part)
    probe_total = jnp.where(core == 0, jnp.stack([part, again]), jnp.stack([again, part]))
    return owned, probe_total


def solution(mesh):
    placed = (
        P("pos", "grp", "tile", None),
        P("grp", None, None),
        P("tile", "grp", "pos", None, None),
        P("tile", "grp", "pos"),
        P("tile", "grp", "pos"),
        P("grp", "tile"),
    )
    return jax.shard_map(
        local,
        mesh=mesh,
        in_specs=placed,
        out_specs=(P("pos", "grp", "tile", None), P("grp", None, None)),
        check_vma=False,
    )
```

time: 622 us -> 140 us (0.23)
  waiting for transfers between devices: 363 us -> 46.9 us
  starting transfers between devices: 118 us -> 27.5 us
  matrix products: 69.7 us -> 0 us
  local copies, waits for them, and re-layouts: 28.5 us -> 48.1 us
  between operations: 14.5 us -> 1.43 us
  other arithmetic: 16.2 us -> 7.06 us
  Pallas kernels: 0 us -> 7.72 us
  loops' own time: 7.7 us -> 0 us
    psum x2 -> x0, waiting for transfers between devices: 305 us -> none  [the longest x1 284 us: local(): probe_total = lax.psum(grad_probe, ('tile', 'pos'))]
    ppermute x2 -> x10, starting transfers between devices: 118 us -> 27.5 us  [the longest x3 20 us: local(): lax.ppermute(part, 'tile', [(i, i ^ step) for i in range(peers)])]
    dot_general x64 -> x0, matrix products: 69.7 us -> none  [matdot(): return jnp.dot(left, right, preferred_element_type=jnp.float32)]
    transpose x0 -> x1, local copies, waits for them, and re-layouts: none -> 32 us  [local(): intensity.reshape(slots, size // 2, 2, size // 2, 2)]
    dynamic_update_slice x2 -> x0, local copies, waits for them, and re-layouts: 22.8 us -> none  [visit(): grad_ext = lax.dynamic_update_slice(grad_ext, previous + grad_win, starts)]
    unnamed x8 -> x11, local copies, waits for them, and re-layouts: 0.02 us -> 13.6 us
    all_gather x1 -> x0, waiting for transfers between devices: 12 us -> none  [local(): both_slices = lax.all_gather(object_slices, 'pos', axis=0, tiled=True)]
    pallas_call x0 -> x1, Pallas kernels: none -> 7.72 us  [local(): pl.pallas_call(kernel, out_shape=(jax.ShapeDtypeStruct((2, strip, ny), f3...]
  transfers between devices with their start and end apart: 5 -> 10, of which waited for: 5 -> 7; matrix products, arithmetic and copies ran while one was open for 1% -> 37% of each run, Pallas kernels for 0% -> 0%
where the time goes in v1:
time: 140 us; the launch traced here: 139 us
  local copies, waits for them, and re-layouts  48.1 us (34%)
  waiting for transfers between devices  46.9 us (34%)
  starting transfers between devices  27.5 us (20%)
  Pallas kernels  7.72 us (6%)
  other arithmetic  7.06 us (5%)
  between operations  1.43 us (1%)
    transpose x1, local copies, waits for them, and re-layouts, local(): intensity.reshape(slots, size // 2, 2, size // 2, 2)  32 us
    ppermute x2, waiting for transfers between devices, shift_tile(): lax.ppermute(value, 'tile', [(i, i + by) for i in range(peers) if 0 <= i...  23 us
    ppermute x3, waiting for transfers between devices, local(): lax.ppermute(part, 'tile', [(i, i ^ step) for i in range(peers)])  20.7 us
    ppermute x3, starting transfers between devices, local(): lax.ppermute(part, 'tile', [(i, i ^ step) for i in range(peers)])  20 us
    unnamed x11, local copies, waits for them, and re-layouts  13.6 us
    pallas_call x1, Pallas kernels, local(): pl.pallas_call(kernel, out_shape=(jax.ShapeDtypeStruct((2, strip, ny), f3...  7.72 us
    ppermute x2, starting transfers between devices, shift_tile(): lax.ppermute(value, 'tile', [(i, i + by) for i in range(peers) if 0 <= i...  6.71 us
    ppermute x5, waiting for transfers between devices, swap(): return lax.ppermute(value, 'pos', [(0, 1), (1, 0)])  3.24 us
  transfers between devices with their start and end apart: 10, of which 7 were waited for; matrix products, arithmetic and copies ran while one was open for 37% of the time, Pallas kernels for 0%

profile of v1, /device:TPU:16, one launch (start us, length us, event | category | flops | bytes accessed | tf_op | source)
XLA Modules:
  0.0 138.7 jit_solution(6432303226557475625)
XLA Ops:
  0.6 3.3 %collective-permute-start.1 = (bf16[2,256,512]{2,1,0:T(8,128)(2,1)}, bf16[2,256,512]{2,1,0:T(8,128)(2,1)S(1)}, u32[]{:S(2)}, u32[]{:S(2)}) collective-permute-start(bf16[2,256,512]{2,1,0:T(8,128)(2,1)} %bitcast.20), channel_id=1, source_target_pairs={{2,0},{4,2},{6,4},{8,6},{10,8},{12,10},{14,12},{3,1},{5,3},{7,5},{... | collective-permute-start | bytes 1572872 | tf_op jit(solution)/shard_map/ppermute | solution.py:264
  4.0 0.1 collective-permute-start
  4.0 12.4 %collective-permute-done.1.halo_own_ref = bf16[2,256,512]{2,1,0:T(8,128)(2,1)S(1)} collective-permute-done((bf16[2,256,512]{2,1,0:T(8,128)(2,1)}, bf16[2,256,512]{2,1,0:T(8,128)(2,1)S(1)}, u32[]{:S(2)}, u32[]{:S(2)}) %collective-permute-start.1) | collective-permute-done | bytes 524320 | tf_op jit(solution)/shard_map/ppermute | solution.py:264
  16.4 0.0 copy-start.2
  16.4 0.0 collective-permute-start.2
  17.1 12.6 %copy.12 = bf16[1,8,1,256,256]{1,4,3,2,0:T(8,128)(2,1)} copy(bf16[1,8,1,256,256]{4,3,2,1,0:T(8,128)(2,1)} %param.11) | data formatting | bytes 2097152 | tf_op args[2]
  29.7 0.0 copy-done.2
  29.7 32.0 %copy.13 = bf16[8,2,128,2,128]{4,3,2,1,0:T(2,128)(2,1)S(1)} copy(bf16[8,2,128,2,128]{0,3,4,1,2:T(2,128)(2,1)} %bitcast.18) | data formatting | bytes 2097152 | tf_op jit(solution)/shard_map/transpose | solution.py:279
  61.7 1.5 %reshape.11.meas_ref = bf16[8,256,256]{2,1,0:T(8,128)(2,1)} reshape(bf16[8,2,128,2,128]{4,3,2,1,0:T(2,128)(2,1)S(1)} %copy.13) | data formatting | bytes 2097152 | tf_op jit(solution)/shard_map/reshape | solution.py:279
  63.2 0.6 pad_add_fusion.info_ref
  63.8 0.0 collective-permute-done.other_ref
  63.8 0.0 copy-start.3
  63.8 0.0 collective-permute-done.2.halo_other_ref
  63.8 0.0 copy-start.4
  63.8 0.8 copy-done.3
  64.6 0.2 copy-done.4
  64.8 7.7 %shard_map.104 = (f32[2,256,512]{2,1,0:T(8,128)}, f32[2,256,512]{2,1,0:T(8,128)}, bf16[2,512,512]{2,1,0:T(8,128)(2,1)}, f32[2,256,256]{2,1,0:T(8,128)}) custom-call(s32[8]{0:T(128)} %bitcast.23, s32[8]{0:T(128)} %bitcast.24, s32[2]{0:T(128)} %pad_add_fusion.info_ref, bf16[2,256,512]{2,1,0:T(8,128)(2,1)} %bitcast.22, bf16[2,256,512]{2,1,0:T(8,128)(2,1)} %copy-done.3, ...), custom_call_target="tpu_custom_call" | custom-call | tf_op jit(solution)/shard_map/pallas_call | solution.py:285
  72.5 0.5 collective-permute-start.3
  73.0 1.0 dynamic-slice_bitcast_fusion
  73.9 0.1 collective-permute-start.5
  74.0 1.6 %collective-permute-done.5 = f32[256,256]{1,0:T(8,128)S(1)} collective-permute-done((f32[256,256]{1,0:T(8,128)S(1)}, f32[256,256]{1,0:T(8,128)S(1)}, u32[]{:S(2)}, u32[]{:S(2)}) %collective-permute-start.5) | collective-permute-done | bytes 262176 | tf_op jit(solution)/shard_map/ppermute | solution.py:259
  75.6 1.0 bitcast_add_fusion
  76.6 19.9 %collective-permute-start.6 = (f32[256,256]{1,0:T(8,128)S(1)}, f32[256,256]{1,0:T(8,128)S(1)}, u32[]{:S(2)}, u32[]{:S(2)}) collective-permute-start(f32[256,256]{1,0:T(8,128)S(1)} %bitcast_add_fusion), channel_id=1, source_target_pairs={{0,2},{2,0},{4,6},{6,4},{8,10},{10,8},{12,14},{14,12},{1,3},{3,1},... | collective-permute-start | bytes 786440 | tf_op jit(solution)/shard_map/ppermute | solution.py:322
  96.5 6.8 %collective-permute-done.6 = f32[256,256]{1,0:T(8,128)S(1)} collective-permute-done((f32[256,256]{1,0:T(8,128)S(1)}, f32[256,256]{1,0:T(8,128)S(1)}, u32[]{:S(2)}, u32[]{:S(2)}) %collective-permute-start.6) | collective-permute-done | bytes 262176 | tf_op jit(solution)/shard_map/ppermute | solution.py:322
  103.4 0.0 copy-start.1
  103.4 0.1 collective-permute-start.7
  103.4 8.0 %collective-permute-done.7 = f32[256,256]{1,0:T(8,128)S(1)} collective-permute-done((f32[256,256]{1,0:T(8,128)S(1)}, f32[256,256]{1,0:T(8,128)S(1)}, u32[]{:S(2)}, u32[]{:S(2)}) %collective-permute-start.7) | collective-permute-done | bytes 262176 | tf_op jit(solution)/shard_map/ppermute | solution.py:322
  111.5 0.1 collective-permute-start.8
  111.6 0.0 collective-permute-done.3
  111.6 0.3 convert_element_type.9
  111.9 0.0 copy-done.1
  111.9 0.0 copy-start
  111.9 0.9 fusion
  112.8 3.4 %collective-permute-start.4 = (bf16[2,256,512]{2,1,0:T(8,128)(2,1)}, bf16[2,256,512]{2,1,0:T(8,128)(2,1)}, u32[]{:S(2)}, u32[]{:S(2)}) collective-permute-start(bf16[2,256,512]{2,1,0:T(8,128)(2,1)} %fusion), channel_id=1, source_target_pairs={{0,2},{2,4},{4,6},{6,8},{8,10},{10,12},{12,14},{1,3},{3,5},{5,7},{... | collective-permute-start | bytes 1572872 | tf_op jit(solution)/shard_map/ppermute | solution.py:264
  116.2 5.9 %collective-permute-done.8 = f32[256,256]{1,0:T(8,128)S(1)} collective-permute-done((f32[256,256]{1,0:T(8,128)S(1)}, f32[256,256]{1,0:T(8,128)S(1)}, u32[]{:S(2)}, u32[]{:S(2)}) %collective-permute-start.8) | collective-permute-done | bytes 262176 | tf_op jit(solution)/shard_map/ppermute | solution.py:322
  122.1 0.1 collective-permute-start.9
  122.2 1.6 %collective-permute-done.9 = f32[256,256]{1,0:T(8,128)} collective-permute-done((f32[256,256]{1,0:T(8,128)S(1)}, f32[256,256]{1,0:T(8,128)}, u32[]{:S(2)}, u32[]{:S(2)}) %collective-permute-start.9) | collective-permute-done | bytes 262176 | tf_op jit(solution)/shard_map/ppermute | solution.py:259
  123.9 1.9 %maximum_select_fusion = f32[2,256,256]{2,1,0:T(8,128)} fusion(f32[1,256,256]{2,1,0:T(8,128)} %bitcast.12, f32[1,256,256]{2,1,0:T(8,128)S(1)} %bitcast.19, pred[]{:T(512)S(6)} %eq.3), kind=kLoop, calls=%fused_computation.5 | loop fusion | flops 393216 | bytes 1048577 | tf_op jit(solution)/shard_map/jit(_where)/select_n | solution.py:326
  125.7 10.6 %collective-permute-done.4 = bf16[2,256,512]{2,1,0:T(8,128)(2,1)} collective-permute-done((bf16[2,256,512]{2,1,0:T(8,128)(2,1)}, bf16[2,256,512]{2,1,0:T(8,128)(2,1)}, u32[]{:S(2)}, u32[]{:S(2)}) %collective-permute-start.4) | collective-permute-done | bytes 524320 | tf_op jit(solution)/shard_map/ppermute | solution.py:264
  136.4 0.0 copy-done
  136.4 2.3 %fusion.2 = f32[1,2,256,512]{3,2,1,0:T(8,128)} fusion(f32[2,256,512]{2,1,0:T(8,128)S(1)} %copy-done, f32[2,512,512]{2,1,0:T(8,128)S(1)} %convert_element_type.9, bf16[2,256,512]{2,1,0:T(8,128)(2,1)} %collective-permute-done.4), kind=kLoop, calls=%fused_computation.4 | loop fusion | flops 786432 | bytes 3670016 | tf_op jit(solution)/shard_map/broadcast_in_dim | solution.py:313
  (3 shorter events, 0.1 us)
Async XLA Ops:
  0.6 15.8 %collective-permute-start.1 = (bf16[2,256,512]{2,1,0:T(8,128)(2,1)}, bf16[2,256,512]{2,1,0:T(8,128)(2,1)S(1)}, u32[]{:S(2)}, u32[]{:S(2)}) collective-permute-start(bf16[2,256,512]{2,1,0:T(8,128)(2,1)} %bitcast.20), channel_id=1, source_target_pairs={{2,0},{4,2},{6,4},{8,6},{10,8},{12,10},{14,12},{3,1},{5,3},{7,5},{... | collective-permute-start | bytes 1572872 | tf_op jit(solution)/shard_map/ppermute | solution.py:264
  4.0 59.8 %collective-permute-start = (bf16[2,256,512]{2,1,0:T(8,128)(2,1)}, bf16[2,256,512]{2,1,0:T(8,128)(2,1)S(1)}, u32[]{:S(2)}, u32[]{:S(2)}) collective-permute-start(bf16[2,256,512]{2,1,0:T(8,128)(2,1)} %bitcast.21), channel_id=1, source_target_pairs={{0,1},{1,0},{2,3},{3,2},{4,5},{5,4},{6,7},{7,6},{8,9},{9,8},{10,11... | collective-permute-start | bytes 1572872 | tf_op jit(solution)/shard_map/ppermute | solution.py:259
  16.4 13.3 %copy-start.2 = (bf16[2,256,512]{2,1,0:T(8,128)(2,1)}, bf16[2,256,512]{2,1,0:T(8,128)(2,1)S(1)}, u32[]{:S(2)}) copy-start(bf16[2,256,512]{2,1,0:T(8,128)(2,1)S(1)} %collective-permute-done.1.halo_own_ref) | copy-start | bytes 1572868
  16.4 47.4 %collective-permute-start.2 = (bf16[2,256,512]{2,1,0:T(8,128)(2,1)S(1)}, bf16[2,256,512]{2,1,0:T(8,128)(2,1)S(1)}, u32[]{:S(2)}, u32[]{:S(2)}) collective-permute-start(bf16[2,256,512]{2,1,0:T(8,128)(2,1)S(1)} %collective-permute-done.1.halo_own_ref), channel_id=1, source_target_pairs={{0,1},{1,0},{2,3},{3,2},{4,5},{5,4},{6,7},{7,6},{8,9},{9,8},{10,11... | collective-permute-start | bytes 1572872 | tf_op jit(solution)/shard_map/ppermute | solution.py:259
  63.8 0.8 copy-start.3
  63.8 1.0 copy-start.4
  72.5 39.1 %collective-permute-start.3 = (bf16[2,512,512]{2,1,0:T(8,128)(2,1)}, bf16[2,512,512]{2,1,0:T(8,128)(2,1)S(1)}, u32[]{:S(2)}, u32[]{:S(2)}) collective-permute-start(bf16[2,512,512]{2,1,0:T(8,128)(2,1)} %get-tuple-element.7), channel_id=1, source_target_pairs={{0,1},{1,0},{2,3},{3,2},{4,5},{5,4},{6,7},{7,6},{8,9},{9,8},{10,11... | collective-permute-start | bytes 3145736 | tf_op jit(solution)/shard_map/ppermute | solution.py:259
  73.9 1.7 %collective-permute-start.5 = (f32[256,256]{1,0:T(8,128)S(1)}, f32[256,256]{1,0:T(8,128)S(1)}, u32[]{:S(2)}, u32[]{:S(2)}) collective-permute-start(f32[256,256]{1,0:T(8,128)S(1)} %dynamic-slice_bitcast_fusion), channel_id=1, source_target_pairs={{0,1},{1,0},{2,3},{3,2},{4,5},{5,4},{6,7},{7,6},{8,9},{9,8},{10,11... | collective-permute-start | bytes 786440 | tf_op jit(solution)/shard_map/ppermute | solution.py:259
  76.6 26.7 %collective-permute-start.6 = (f32[256,256]{1,0:T(8,128)S(1)}, f32[256,256]{1,0:T(8,128)S(1)}, u32[]{:S(2)}, u32[]{:S(2)}) collective-permute-start(f32[256,256]{1,0:T(8,128)S(1)} %bitcast_add_fusion), channel_id=1, source_target_pairs={{0,2},{2,0},{4,6},{6,4},{8,10},{10,8},{12,14},{14,12},{1,3},{3,1},... | collective-permute-start | bytes 786440 | tf_op jit(solution)/shard_map/ppermute | solution.py:322
  103.4 8.5 %copy-start.1 = (f32[2,256,512]{2,1,0:T(8,128)S(1)}, f32[2,256,512]{2,1,0:T(8,128)}, u32[]{:S(2)}) copy-start(f32[2,256,512]{2,1,0:T(8,128)} %get-tuple-element.8) | copy-start | bytes 3145732
  103.4 8.1 %collective-permute-start.7 = (f32[256,256]{1,0:T(8,128)S(1)}, f32[256,256]{1,0:T(8,128)S(1)}, u32[]{:S(2)}, u32[]{:S(2)}) collective-permute-start(f32[256,256]{1,0:T(8,128)S(1)} %add.40), channel_id=1, source_target_pairs={{0,4},{2,6},{4,0},{6,2},{8,12},{10,14},{12,8},{14,10},{1,5},{3,7},... | collective-permute-start | bytes 786440 | tf_op jit(solution)/shard_map/ppermute | solution.py:322
  111.5 10.6 %collective-permute-start.8 = (f32[256,256]{1,0:T(8,128)S(1)}, f32[256,256]{1,0:T(8,128)S(1)}, u32[]{:S(2)}, u32[]{:S(2)}) collective-permute-start(f32[256,256]{1,0:T(8,128)S(1)} %add.41), channel_id=1, source_target_pairs={{0,8},{2,10},{4,12},{6,14},{8,0},{10,2},{12,4},{14,6},{1,9},{3,11}... | collective-permute-start | bytes 786440 | tf_op jit(solution)/shard_map/ppermute | solution.py:322
  111.9 24.5 %copy-start = (f32[2,256,512]{2,1,0:T(8,128)S(1)}, f32[2,256,512]{2,1,0:T(8,128)}, u32[]{:S(2)}) copy-start(f32[2,256,512]{2,1,0:T(8,128)} %get-tuple-element.6) | copy-start | bytes 3145732
  112.8 23.6 %collective-permute-start.4 = (bf16[2,256,512]{2,1,0:T(8,128)(2,1)}, bf16[2,256,512]{2,1,0:T(8,128)(2,1)}, u32[]{:S(2)}, u32[]{:S(2)}) collective-permute-start(bf16[2,256,512]{2,1,0:T(8,128)(2,1)} %fusion), channel_id=1, source_target_pairs={{0,2},{2,4},{4,6},{6,8},{8,10},{10,12},{12,14},{1,3},{3,5},{5,7},{... | collective-permute-start | bytes 1572872 | tf_op jit(solution)/shard_map/ppermute | solution.py:264
  122.1 1.7 %collective-permute-start.9 = (f32[256,256]{1,0:T(8,128)S(1)}, f32[256,256]{1,0:T(8,128)}, u32[]{:S(2)}, u32[]{:S(2)}) collective-permute-start(f32[256,256]{1,0:T(8,128)S(1)} %add_multiply_fusion), channel_id=1, source_target_pairs={{0,1},{1,0},{2,3},{3,2},{4,5},{5,4},{6,7},{7,6},{8,9},{9,8},{10,11... | collective-permute-start | bytes 786440 | tf_op jit(solution)/shard_map/ppermute | solution.py:259

commit v2 on v0

v2 whole, which is shorter than its diff:
```python
import math

import jax
import jax.numpy as jnp
import ml_dtypes
import numpy as np
from jax import lax
from jax.experimental import pallas as pl
from jax.experimental.pallas import tpu as pltpu
from jax.sharding import PartitionSpec as P

BAND = 32
LANES = 128
CHUNK = 16
WIN_CHUNK = 32
GROUP = 4
VMEM_BYTES = 40 * 1024 * 1024
f32 = jnp.float32
bf16 = jnp.bfloat16


def tables(size):
    index = np.arange(size, dtype=np.int32)
    offset = index[:, None] - index[None, :]
    inside = (np.abs(offset) <= BAND).astype(np.float32)
    offset_f = offset.astype(np.float32)
    phase = (np.float32(math.pi) * offset_f * offset_f / np.float32(2.0 * BAND)).astype(np.float32)
    scale = np.float32(1.0 / math.sqrt(2 * BAND + 1))
    prop_re = np.cos(phase) * inside * scale
    prop_im = np.sin(phase) * inside * scale
    product = (index[:, None] * index[None, :]) % size
    angle = (np.float32(-2.0 * math.pi) * product.astype(np.float32) / np.float32(size)).astype(np.float32)
    root = np.float32(math.sqrt(size))
    return prop_re, prop_im, np.cos(angle) / root, np.sin(angle) / root


def packed(mat_re, mat_im):
    n, k = mat_re.shape
    upper = np.concatenate([mat_re, -mat_im], axis=1).reshape(n // CHUNK, 1, CHUNK, 2 * k)
    lower = np.concatenate([mat_im, mat_re], axis=1).reshape(n // CHUNK, 1, CHUNK, 2 * k)
    both = np.concatenate([upper, lower], axis=1).reshape(2 * n, 2 * k)
    return both.astype(np.float32).astype(ml_dtypes.bfloat16)


def constants(size):
    half = size // 2
    kr, ki, fr, fi = tables(size)
    near, far = half + BAND, half - BAND
    prop = [
        packed(kr[:near, :half], ki[:near, :half]),
        packed(kr[far:, half:], ki[far:, half:]),
        packed(kr[:near, :half], -ki[:near, :half]),
        packed(kr[far:, half:], -ki[far:, half:]),
    ]
    four = [
        packed(fr[0::2, :half], fi[0::2, :half]),
        packed(fr[1::2, :half], fi[1::2, :half]),
        packed(fr[:half, 0::2], -fi[:half, 0::2]),
        packed(fr[:half, 1::2], -fi[:half, 1::2]),
    ]
    order = np.concatenate([np.arange(0, size, 2), np.arange(1, size, 2)])
    perm = np.eye(size, dtype=np.float32)[order].astype(ml_dtypes.bfloat16)
    return np.stack(prop), np.stack(four), perm


def nt(left, right):
    return lax.dot_general(left, right, (((1,), (1,)), ((), ())), preferred_element_type=f32)


def banded(prop_ref, base, source):
    size = source.shape[1] // 2
    skip = (size // 2 - BAND) // CHUNK
    stop = (size // 2 + BAND) // CHUNK
    first = nt(prop_ref[base], source[:, :size])
    second = nt(prop_ref[base + 1], source[:, size:])

    def at(j):
        out = []
        for part in range(2):
            value = None
            if j < stop:
                lo = (2 * j + part) * CHUNK
                value = first[lo : lo + CHUNK]
            if j >= skip:
                lo = (2 * (j - skip) + part) * CHUNK
                more = second[lo : lo + CHUNK]
                value = more if value is None else value + more
            out.append(value)
        return out

    return at


def halves(four_ref, base, source):
    size = source.shape[1] // 2
    first = nt(four_ref[base], source[:, :size])
    second = nt(four_ref[base + 1], source[:, size:])

    def at(j):
        lo = 2 * j * CHUNK
        return (
            (first[lo : lo + CHUNK], first[lo + CHUNK : lo + 2 * CHUNK]),
            (second[lo : lo + CHUNK], second[lo + CHUNK : lo + 2 * CHUNK]),
        )

    return at


def put(target, lo, re, im):
    half = re.shape[1] // 2
    target[lo : lo + CHUNK, :] = jnp.concatenate(
        [re[:, :half], im[:, :half], re[:, half:], im[:, half:]], axis=1
    ).astype(bf16)


def put_butterfly(target, lo, re, im):
    half = re.shape[1] // 2
    target[lo : lo + CHUNK, :] = jnp.concatenate(
        [
            re[:, :half] + re[:, half:],
            im[:, :half] + im[:, half:],
            re[:, :half] - re[:, half:],
            im[:, :half] - im[:, half:],
        ],
        axis=1,
    ).astype(bf16)


class Place:
    def __init__(self, row, col):
        self.row = row
        self.block = lax.shift_right_logical(col, 7)
        self.shift = jnp.bitwise_and(col, LANES - 1)


def fill(ext, core, strips, halos):
    strip = strips[0].shape[1]
    for side in range(2):

        @pl.when(core == side)
        def _():
            for part in range(2):
                for block in range(strips[side].shape[2] // LANES):
                    lanes = slice(block * LANES, (block + 1) * LANES)
                    ext[part, block, :strip, :] = strips[side][part, :, lanes].astype(f32)
                    ext[part, block, strip:, :] = halos[side][part, :, lanes].astype(f32)


def window(ext, win, place):
    size = win.shape[1]
    back = jnp.bitwise_and(LANES - place.shift, LANES - 1)
    keep = lax.broadcasted_iota(jnp.int32, (WIN_CHUNK, LANES), 1) < LANES - place.shift
    for lo in range(0, size, WIN_CHUNK):
        span = slice(lo, lo + WIN_CHUNK)
        for part in range(2):
            loaded = [
                pltpu.roll(ext[part, place.block + i, pl.ds(place.row + lo, WIN_CHUNK), :], back, 1)
                for i in range(3)
            ]
            win[part, span, :LANES] = jnp.where(keep, loaded[0], loaded[1])
            win[part, span, LANES:] = jnp.where(keep, loaded[1], loaded[2])


def scatter(acc, place, lo, parts):
    low = lax.broadcasted_iota(jnp.int32, (CHUNK, LANES), 1) < place.shift
    for part, value in enumerate(parts):
        left = pltpu.roll(value[:, :LANES], place.shift, 1)
        right = pltpu.roll(value[:, LANES:], place.shift, 1)
        pieces = (jnp.where(low, 0.0, left), jnp.where(low, left, right), jnp.where(low, right, 0.0))
        for i, piece in enumerate(pieces):
            at = (part, place.block + i, pl.ds(place.row + lo, CHUNK), slice(None))
            acc[at] = acc[at] + piece


def emit(acc, strip_ref, tail_ref, send_strip_ref, send_tail_ref):
    strip, ny = strip_ref.shape[1:]
    for part in range(2):
        for block in range(ny // LANES):
            lanes = slice(block * LANES, (block + 1) * LANES)
            upper = acc[part, block, :strip, :]
            lower = acc[part, block, strip:, :]
            strip_ref[part, :, lanes] = upper
            tail_ref[part, :, lanes] = lower
            send_strip_ref[part, :, lanes] = upper.astype(bf16)
            send_tail_ref[part, :, lanes] = lower.astype(bf16)


def members(step, live, slots):
    for g in range(GROUP):
        slot = step * GROUP + g
        yield jnp.minimum(slot, live - 1), jnp.where(slot < live, slot, slots + g - 1), slot < live


def prepare_kernel(meas_ref, perm_ref, own_ref, out_ref, own_out_ref):
    own_out_ref[...] = own_ref[...]
    perm = perm_ref[...]
    for slot in range(meas_ref.shape[0]):
        rows = jnp.dot(perm, meas_ref[slot], preferred_element_type=f32).astype(bf16)
        out_ref[slot] = nt(rows, perm).astype(bf16)


def forward_kernel(
    rows_ref, cols_ref, info_ref,
    own_ref, other_ref, halo_ref, passed_ref, probe_ref, prop_ref,
    wave_ref,
    ext, win, x_a, x_b, pro,
):
    size = probe_ref.shape[1]
    steps = size // CHUNK
    core, live = info_ref[0], info_ref[1]
    slots = wave_ref.shape[0]
    fill(ext, core, (own_ref, other_ref), (halo_ref, passed_ref))
    pro[...] = probe_ref[...].astype(f32)

    def visit(step, _):
        group = list(members(step, live, slots))
        for g, (slot, _, _) in enumerate(group):
            window(ext, win.at[g], Place(rows_ref[slot], cols_ref[slot]))
            for j in range(steps):
                span = slice(j * CHUNK, (j + 1) * CHUNK)
                pr, pi = pro[0, span], pro[1, span]
                wr, wi = win[g, 0, span], win[g, 1, span]
                put(x_a.at[g], j * CHUNK, pr * wr - pi * wi, pr * wi + pi * wr)
        for g in range(GROUP):
            at = banded(prop_ref, 0, x_a[g])
            for j in range(steps):
                put(x_b.at[g], j * CHUNK, *at(j))
        for g, (slot, _, _) in enumerate(group):
            at = banded(prop_ref, 0, x_b[g])
            for j in range(steps):
                re, im = at(j)
                span = slice(j * CHUNK, (j + 1) * CHUNK)
                wave_ref[slot, 0, span] = re.astype(bf16)
                wave_ref[slot, 1, span] = im.astype(bf16)
        return 0

    lax.fori_loop(0, (live + GROUP - 1) // GROUP, visit, 0)


def detector_kernel(
    rows_ref, cols_ref, info_ref,
    own_ref, other_ref, halo_ref, passed_ref, wave_ref, meas_ref, prop_ref, four_ref,
    back_ref, strip_ref, tail_ref, send_strip_ref, send_tail_ref,
    ext, acc, win, x_a, x_b,
):
    size = meas_ref.shape[1]
    half = size // 2
    steps = size // CHUNK
    core, live = info_ref[0], info_ref[1]
    slots = wave_ref.shape[0]
    fill(ext, core, (other_ref, own_ref), (passed_ref, halo_ref))
    acc[...] = jnp.zeros(acc.shape, f32)

    def visit(step, _):
        group = list(members(step, live, slots))
        places = [Place(rows_ref[slot], cols_ref[slot]) for slot, _, _ in group]
        for g, (slot, _, _) in enumerate(group):
            window(ext, win.at[g], places[g])
            for j in range(steps):
                span = slice(j * CHUNK, (j + 1) * CHUNK)
                br, bi = wave_ref[slot, 0, span].astype(f32), wave_ref[slot, 1, span].astype(f32)
                wr, wi = win[g, 0, span], win[g, 1, span]
                put_butterfly(x_a.at[g], j * CHUNK, br * wr - bi * wi, br * wi + bi * wr)
        for g in range(GROUP):
            at = halves(four_ref, 0, x_a[g])
            for j in range(steps // 2):
                even, odd = at(j)
                put_butterfly(x_b.at[g], j * CHUNK, *even)
                put_butterfly(x_b.at[g], half + j * CHUNK, *odd)
        for g, (slot, _, valid) in enumerate(group):
            at = halves(four_ref, 0, x_b[g])
            factor = jnp.where(valid, 1.0, 0.0).astype(f32)
            for j in range(steps // 2):
                for side, (re, im) in enumerate(at(j)):
                    lo = side * half + j * CHUNK
                    misfit = re * re + im * im - meas_ref[slot, lo : lo + CHUNK, :].astype(f32)
                    misfit = misfit * factor
                    put(x_a.at[g], lo, misfit * re, misfit * im)
        for g in range(GROUP):
            at = halves(four_ref, 2, x_a[g])
            for j in range(steps // 2):
                (er, ei), (dr, di) = at(j)
                put(x_b.at[g], j * CHUNK, er + dr, ei + di)
                put(x_b.at[g], half + j * CHUNK, er - dr, ei - di)
        for g, (slot, target, _) in enumerate(group):
            at = halves(four_ref, 2, x_b[g])
            for j in range(steps // 2):
                (er, ei), (dr, di) = at(j)
                for side in range(2):
                    lo = side * half + j * CHUNK
                    span = slice(lo, lo + CHUNK)
                    re, im = (er + dr, ei + di) if side == 0 else (er - dr, ei - di)
                    br, bi = wave_ref[slot, 0, span].astype(f32), wave_ref[slot, 1, span].astype(f32)
                    wr, wi = win[g, 0, span], win[g, 1, span]
                    put(back_ref.at[target], lo, re * wr + im * wi, im * wr - re * wi)
                    scatter(acc, places[g], lo, (re * br + im * bi, im * br - re * bi))
        return 0

    lax.fori_loop(0, (live + GROUP - 1) // GROUP, visit, 0)
    emit(acc, strip_ref, tail_ref, send_strip_ref, send_tail_ref)


def backward_kernel(
    rows_ref, cols_ref, info_ref,
    own_ref, other_ref, halo_ref, passed_ref, back_ref, probe_ref, prop_ref,
    strip_ref, tail_ref, send_strip_ref, send_tail_ref, mine_ref, theirs_ref,
    ext, acc, win, x_b, pro, pacc,
):
    size = probe_ref.shape[1]
    steps = size // CHUNK
    core, live = info_ref[0], info_ref[1]
    slots = back_ref.shape[0] - GROUP + 1
    fill(ext, core, (own_ref, other_ref), (halo_ref, passed_ref))
    acc[...] = jnp.zeros(acc.shape, f32)
    pacc[...] = jnp.zeros(pacc.shape, f32)
    pro[...] = probe_ref[...].astype(f32)

    def visit(step, _):
        group = list(members(step, live, slots))
        places = [Place(rows_ref[slot], cols_ref[slot]) for slot, _, _ in group]
        for g, (slot, source, _) in enumerate(group):
            window(ext, win.at[g], places[g])
            at = banded(prop_ref, 2, back_ref[source])
            for j in range(steps):
                put(x_b.at[g], j * CHUNK, *at(j))
        for g in range(GROUP):
            at = banded(prop_ref, 2, x_b[g])
            for j in range(steps):
                lo = j * CHUNK
                span = slice(lo, lo + CHUNK)
                re, im = at(j)
                pr, pi = pro[0, span], pro[1, span]
                wr, wi = win[g, 0, span], win[g, 1, span]
                scatter(acc, places[g], lo, (re * pr + im * pi, im * pr - re * pi))
                pacc[0, span] = pacc[0, span] + (re * wr + im * wi)
                pacc[1, span] = pacc[1, span] + (im * wr - re * wi)
        return 0

    lax.fori_loop(0, (live + GROUP - 1) // GROUP, visit, 0)
    emit(acc, strip_ref, tail_ref, send_strip_ref, send_tail_ref)
    mine_ref[...] = pacc[core]
    theirs_ref[...] = pacc[1 - core].astype(bf16)


def swap(value):
    return lax.ppermute(value, "pos", [(0, 1), (1, 0)])


def across(value, start):
    return lax.ppermute(value, "pos", [(start, 1 - start)])


def shift_tile(value, core, by):
    peers, cores = lax.axis_size("tile"), lax.axis_size("pos")
    pairs = [(i * cores + core, (i + by) * cores + core) for i in range(peers) if 0 <= i + by < peers]
    return lax.ppermute(value, ("tile", "pos"), pairs)


def sum_over_tiles(value):
    peers = lax.axis_size("tile")
    step = 1
    while step < peers:
        half = value.astype(bf16)
        got = lax.ppermute(half, "tile", [(i, i ^ step) for i in range(peers)])
        value = half.astype(f32) + got.astype(f32)
        step *= 2
    return value


def call(body, results, operands, scalars, scratch, flops):
    vmem = pl.BlockSpec(memory_space=pltpu.VMEM)
    smem = pl.BlockSpec(memory_space=pltpu.SMEM)
    moved = sum(math.prod(x.shape) * x.dtype.itemsize for x in list(operands) + list(results))
    return pl.pallas_call(
        body,
        out_shape=tuple(results),
        in_specs=[smem] * len(scalars) + [vmem] * len(operands),
        out_specs=(vmem,) * len(results),
        scratch_shapes=scratch,
        cost_estimate=pl.CostEstimate(flops=flops, bytes_accessed=moved, transcendentals=0),
        compiler_params=pltpu.CompilerParams(vmem_limit_bytes=VMEM_BYTES),
    )(*scalars, *operands)


def local(object_slices, probe, intensity, scan_rows, scan_cols, counts):
    strip, ny = object_slices.shape[2:]
    size = probe.shape[1]
    slots = intensity.shape[1]
    cores = lax.axis_size("pos")
    core = lax.axis_index("pos")
    prop, four, perm = (jnp.asarray(t) for t in constants(size))
    sds = jax.ShapeDtypeStruct
    own = object_slices[0]
    live = jnp.minimum(jnp.maximum(counts[0, 0] - core + cores - 1, 0) // cores, slots)
    info = jnp.stack([core, live]).astype(jnp.int32)
    scalars = (scan_rows[0, :, 0], scan_cols[0, :, 0], info)
    blocks = ny // LANES + 1
    cube = 2 * size**3

    halo0 = shift_tile(own, 0, -1)
    other = swap(own)
    passed0 = across(halo0, 0)
    measured, own_later = call(
        prepare_kernel,
        (sds((slots, size, size), bf16), sds(own.shape, bf16)),
        (intensity.reshape(slots, size, size), perm, own),
        (), [], 2 * slots * cube,
    )
    halo1 = shift_tile(own_later, 1, -1)
    passed1 = across(halo1, 1)

    ext = pltpu.VMEM((2, blocks, 2 * strip, LANES), f32)
    win = pltpu.VMEM((GROUP, 2, size, size), f32)
    half_wave = pltpu.VMEM((GROUP, size, 2 * size), bf16)
    full = pltpu.VMEM((2, size, size), f32)
    slice_outs = (
        sds((2, strip, ny), f32), sds((2, strip, ny), f32), sds((2, strip, ny), bf16), sds((2, strip, ny), bf16),
    )
    (wave,) = call(
        forward_kernel,
        (sds((slots, 2, size, size), bf16),),
        (own, other, halo0, passed0, probe, prop),
        scalars, [ext, win, half_wave, half_wave, full], 5 * slots * cube,
    )
    back, strip1, tail1, send_strip1, send_tail1 = call(
        detector_kernel,
        (sds((slots + GROUP - 1, size, 2 * size), bf16),) + slice_outs,
        (own, other, halo1, passed1, wave, measured, prop, four),
        scalars, [ext, ext, win, half_wave, half_wave], 8 * slots * cube,
    )
    got_tail1 = across(send_tail1, 0).astype(f32)
    above1 = shift_tile((tail1 + got_tail1).astype(bf16), 1, 1)
    got_strip1 = across(send_strip1, 0)
    strip0, tail0, send_strip0, send_tail0, mine, theirs = call(
        backward_kernel,
        slice_outs + (sds((size, size), f32), sds((size, size), bf16)),
        (own, other, halo0, passed0, back, probe, prop),
        scalars, [ext, ext, win, half_wave, full, full], 5 * slots * cube,
    )
    part = mine + swap(theirs).astype(f32)
    got_tail0 = across(send_tail0, 1).astype(f32)
    above0 = shift_tile((tail0 + got_tail0).astype(bf16), 0, 1)
    got_strip0 = across(send_strip0, 1)
    owned = jnp.where(core == 0, strip0, strip1)
    for more in (got_strip0, got_strip1, above0, above1):
        owned = owned + more.astype(f32)

    total_slots = lax.axis_size("tile") * slots * cores
    part = sum_over_tiles(part) / math.sqrt(total_slots)
    again = swap(part)
    probe_total = jnp.where(core == 0, jnp.stack([part, again]), jnp.stack([again, part]))
    return owned[None], probe_total


def solution(mesh):
    placed = (
        P("pos", "grp", "tile", None),
        P("grp", None, None),
        P("tile", "grp", "pos", None, None),
        P("tile", "grp", "pos"),
        P("tile", "grp", "pos"),
        P("grp", "tile"),
    )
    return jax.shard_map(
        local,
        mesh=mesh,
        in_specs=placed,
        out_specs=(P("pos", "grp", "tile", None), P("grp", None, None)),
        check_vma=False,
    )
```

time: 622 us -> 84.7 us (0.14)
  waiting for transfers between devices: 363 us -> 20.7 us
  starting transfers between devices: 118 us -> 25.9 us
  matrix products: 69.7 us -> 0 us
  Pallas kernels: 0 us -> 21.9 us
  local copies, waits for them, and re-layouts: 28.5 us -> 9.33 us
  between operations: 14.5 us -> 1.55 us
  other arithmetic: 16.2 us -> 4.54 us
  loops' own time: 7.7 us -> 0 us
    psum x2 -> x0, waiting for transfers between devices: 305 us -> none  [the longest x1 284 us: local(): probe_total = lax.psum(grad_probe, ('tile', 'pos'))]
    ppermute x2 -> x16, starting transfers between devices: 118 us -> 25.9 us  [the longest x6 11.1 us: across(): return lax.ppermute(value, 'pos', [(start, 1 - start)])]
    dot_general x64 -> x0, matrix products: 69.7 us -> none  [matdot(): return jnp.dot(left, right, preferred_element_type=jnp.float32)]
    ppermute x2 -> x16, waiting for transfers between devices: 45.2 us -> 20.7 us  [the longest x4 13.9 us: shift_tile(): return lax.ppermute(value, ('tile', 'pos'), pairs)]
    dynamic_update_slice x2 -> x0, local copies, waits for them, and re-layouts: 22.8 us -> none  [visit(): grad_ext = lax.dynamic_update_slice(grad_ext, previous + grad_win, starts)]
    pallas_call x0 -> x4, Pallas kernels: none -> 21.9 us  [call(): pl.pallas_call(body, out_shape=tuple(results), in_specs=[smem] * len(scal...]
    all_gather x1 -> x0, waiting for transfers between devices: 12 us -> none  [local(): both_slices = lax.all_gather(object_slices, 'pos', axis=0, tiled=True)]
    unnamed x8 -> x36, local copies, waits for them, and re-layouts: 0.02 us -> 9.33 us
  transfers between devices with their start and end apart: 5 -> 16, of which waited for: 5 -> 6; matrix products, arithmetic and copies ran while one was open for 1% -> 2% of each run, Pallas kernels for 0% -> 8%
where the time goes in v2:
time: 84.7 us; the launch traced here: 83.9 us
  starting transfers between devices  25.9 us (31%)
  Pallas kernels  21.9 us (26%)
  waiting for transfers between devices  20.7 us (24%)
  local copies, waits for them, and re-layouts  9.33 us (11%)
  other arithmetic  4.54 us (5%)
  between operations  1.55 us (2%)
    pallas_call x4, Pallas kernels, call(): pl.pallas_call(body, out_shape=tuple(results), in_specs=[smem] * len(scal...  21.9 us
    ppermute x4, waiting for transfers between devices, shift_tile(): return lax.ppermute(value, ('tile', 'pos'), pairs)  13.9 us
    ppermute x6, starting transfers between devices, across(): return lax.ppermute(value, 'pos', [(start, 1 - start)])  11.1 us
    unnamed x36, local copies, waits for them, and re-layouts  9.33 us
    ppermute x4, starting transfers between devices, shift_tile(): return lax.ppermute(value, ('tile', 'pos'), pairs)  8.09 us
    ppermute x3, waiting for transfers between devices, sum_over_tiles(): got = lax.ppermute(half, 'tile', [(i, i ^ step) for i in range(peers)])  4.26 us
    ppermute x3, starting transfers between devices, sum_over_tiles(): got = lax.ppermute(half, 'tile', [(i, i ^ step) for i in range(peers)])  3.62 us
    ppermute x3, starting transfers between devices, swap(): return lax.ppermute(value, 'pos', [(0, 1), (1, 0)])  3.1 us
  transfers between devices with their start and end apart: 16, of which 6 were waited for; matrix products, arithmetic and copies ran while one was open for 2% of the time, Pallas kernels for 8%

profile of v2, /device:TPU:16, one launch (start us, length us, event | category | flops | bytes accessed | tf_op | source)
XLA Modules:
  0.0 83.9 jit_solution(16363879307142081791)
XLA Ops:
  0.6 3.3 %collective-permute-start.1 = (bf16[2,256,512]{2,1,0:T(8,128)(2,1)}, bf16[2,256,512]{2,1,0:T(8,128)(2,1)S(1)}, u32[]{:S(2)}, u32[]{:S(2)}) collective-permute-start(bf16[2,256,512]{2,1,0:T(8,128)(2,1)} %bitcast.5.own_ref), channel_id=1, source_target_pairs={{2,0},{4,2},{6,4},{8,6},{10,8},{12,10},{14,12},{18,16},{20,18},{22... | collective-permute-start | bytes 1572872 | tf_op jit(solution)/shard_map/ppermute | solution.py:356
  4.0 0.0 copy-start.9
  4.0 1.2 %copy-done.9 = bf16[1,8,1,256,256]{4,3,2,1,0:T(8,128)(2,1)S(1)} copy-done((bf16[1,8,1,256,256]{4,3,2,1,0:T(8,128)(2,1)S(1)}, bf16[1,8,1,256,256]{4,3,2,1,0:T(8,128)(2,1)}, u32[]{:S(2)}) %copy-start.9) | copy-done | bytes 1048600
  5.2 0.9 %copy-done.15 = bf16[256,256]{1,0:T(8,128)(2,1)S(1)} copy-done((bf16[256,256]{1,0:T(8,128)(2,1)S(1)}, bf16[256,256]{1,0:T(8,128)(2,1)}, u32[]{:S(2)}) %copy-start.15) | copy-done | bytes 131096
  6.1 1.9 %shard_map.104 = (bf16[8,256,256]{2,1,0:T(8,128)(2,1)S(1)}, bf16[2,256,512]{2,1,0:T(8,128)(2,1)S(1)}) custom-call(bf16[8,256,256]{2,1,0:T(8,128)(2,1)S(1)} %bitcast.19, bf16[256,256]{1,0:T(8,128)(2,1)S(1)} %copy-done.15, bf16[2,256,512]{2,1,0:T(8,128)(2,1)} %bitcast.5.own_ref), custom_call_target="tpu_custom_call" | custom-call | flops 536870912 | bytes 3276800 | tf_op jit(solution)/shard_map/pallas_call | solution.py:374
  8.0 0.0 copy-start.16
  8.1 1.0 %copy-done.16 = bf16[8,256,256]{2,1,0:T(8,128)(2,1)} copy-done((bf16[8,256,256]{2,1,0:T(8,128)(2,1)}, bf16[8,256,256]{2,1,0:T(8,128)(2,1)S(1)}, u32[]{:S(2)}) %copy-start.16) | copy-done | bytes 1048600
  9.0 0.8 collective-permute-start.3
  9.8 0.1 collective-permute-start
  9.9 3.0 %collective-permute-done.1.halo_ref = bf16[2,256,512]{2,1,0:T(8,128)(2,1)S(1)} collective-permute-done((bf16[2,256,512]{2,1,0:T(8,128)(2,1)}, bf16[2,256,512]{2,1,0:T(8,128)(2,1)S(1)}, u32[]{:S(2)}, u32[]{:S(2)}) %collective-permute-start.1) | collective-permute-done | bytes 524320 | tf_op jit(solution)/shard_map/ppermute | solution.py:356
  12.9 1.3 %collective-permute-start.2 = (bf16[2,256,512]{2,1,0:T(8,128)(2,1)S(1)}, bf16[2,256,512]{2,1,0:T(8,128)(2,1)S(1)}, u32[]{:S(2)}, u32[]{:S(2)}) collective-permute-start(bf16[2,256,512]{2,1,0:T(8,128)(2,1)S(1)} %collective-permute-done.1.halo_ref), channel_id=1, source_target_pairs={{0,1},{2,3},{4,5},{6,7},{8,9},{10,11},{12,13},{14,15},{16,17},{18,... | collective-permute-start | bytes 1572872 | tf_op jit(solution)/shard_map/ppermute | solution.py:350
  14.2 0.0 collective-permute-done.3.halo_ref
  14.3 0.0 copy-start.10
  14.3 1.3 %collective-permute-start.4 = (bf16[2,256,512]{2,1,0:T(8,128)(2,1)S(1)}, bf16[2,256,512]{2,1,0:T(8,128)(2,1)S(1)}, u32[]{:S(2)}, u32[]{:S(2)}) collective-permute-start(bf16[2,256,512]{2,1,0:T(8,128)(2,1)S(1)} %collective-permute-done.3.halo_ref), channel_id=1, source_target_pairs={{1,0},{3,2},{5,4},{7,6},{9,8},{11,10},{13,12},{15,14},{17,16},{19,... | collective-permute-start | bytes 1572872 | tf_op jit(solution)/shard_map/ppermute | solution.py:350
  16.2 0.1 pad_add_fusion.info_ref
  16.3 0.0 collective-permute-done.other_ref
  16.3 0.0 collective-permute-done.2.passed_ref
  16.3 1.1 %copy-done = bf16[4,320,256]{2,1,0:T(8,128)(2,1)S(1)} copy-done((bf16[4,320,256]{2,1,0:T(8,128)(2,1)S(1)}, bf16[4,320,256]{2,1,0:T(8,128)(2,1)}, u32[]{:S(2)}) %copy-start) | copy-done | bytes 655384
  17.4 0.9 %copy-done.2 = bf16[2,256,256]{2,1,0:T(8,128)(2,1)S(1)} copy-done((bf16[2,256,256]{2,1,0:T(8,128)(2,1)S(1)}, bf16[2,256,256]{2,1,0:T(8,128)(2,1)}, u32[]{:S(2)}) %copy-start.2) | copy-done | bytes 262168
  18.4 0.7 copy-done.5
  19.0 0.7 copy-done.7
  19.7 4.6 %shard_map.105.wave_ref = bf16[8,2,256,256]{3,2,1,0:T(8,128)(2,1)S(1)} custom-call(s32[8]{0:T(128)S(1)} %bitcast.13, s32[8]{0:T(128)S(1)} %bitcast.16, s32[2]{0:T(128)S(1)} %pad_add_fusion.info_ref, bf16[2,256,512]{2,1,0:T(8,128)(2,1)} %bitcast.5.own_ref, bf16[2,256,512]{2,1,0:T(8,128)(2,1)S(1)} %collective-permute-done.other_ref, ...), custom_call_target="tpu_custom_call" | custom-call | flops 1342177280 | bytes 5111808 | tf_op jit(solution)/shard_map/pallas_call | solution.py:374
  24.3 0.0 collective-permute-done.4.passed_ref
  24.3 0.0 copy-done.10
  24.3 0.0 copy-start.12
  24.3 0.8 copy-done.12
  25.1 0.0 copy-done.1
  25.1 0.0 copy-done.6
  25.1 0.0 copy-done.8
  25.1 0.0 copy-done.14
  25.1 0.0 copy-done.17
  25.1 0.0 copy-start.11
  25.2 1.0 %copy-done.11 = bf16[2,256,512]{2,1,0:T(8,128)(2,1)S(1)} copy-done((bf16[2,256,512]{2,1,0:T(8,128)(2,1)S(1)}, bf16[2,256,512]{2,1,0:T(8,128)(2,1)}, u32[]{:S(2)}) %copy-start.11) | copy-done | bytes 524312
  26.2 1.0 %copy-done.13 = bf16[2,256,512]{2,1,0:T(8,128)(2,1)S(1)} copy-done((bf16[2,256,512]{2,1,0:T(8,128)(2,1)S(1)}, bf16[2,256,512]{2,1,0:T(8,128)(2,1)}, u32[]{:S(2)}) %copy-start.13) | copy-done | bytes 524312
  27.2 8.6 %shard_map.106 = (bf16[11,256,512]{2,1,0:T(8,128)(2,1)S(1)}, f32[2,256,512]{2,1,0:T(8,128)S(1)}, f32[2,256,512]{2,1,0:T(8,128)S(1)}, bf16[2,256,512]{2,1,0:T(8,128)(2,1)}, bf16[2,256,512]{2,1,0:T(8,128)(2,1)S(1)}) custom-call(s32[8]{0:T(128)S(1)} %bitcast.14, s32[8]{0:T(128)S(1)} %bitcast.17, s32[2]{0:T(128)S(1)} %pad_add_fusion.info_ref, ...), custom_call_target="tpu_custom_call" | custom-call | flops 2147483648 | bytes 12451840 | tf_op jit(solution)/shard_map/pallas_call | solution.py:374
  35.8 0.0 copy-done.3
  35.8 6.7 %shard_map.107 = (f32[2,256,512]{2,1,0:T(8,128)S(1)}, f32[2,256,512]{2,1,0:T(8,128)S(1)}, bf16[2,256,512]{2,1,0:T(8,128)(2,1)}, bf16[2,256,512]{2,1,0:T(8,128)(2...) custom-call(s32[8]{0:T(128)S(1)} %bitcast.15, s32[8]{0:T(128)S(1)} %bitcast.18, ...), custom_call_target="tpu_custom_call" | custom-call | flops 1342177280 | bytes 9437184 | tf_op jit(solution)/shard_map/pallas_call | solution.py:374
  42.5 3.0 %collective-permute-start.11 = (bf16[256,256]{1,0:T(8,128)(2,1)S(1)}, bf16[256,256]{1,0:T(8,128)(2,1)S(1)}, u32[]{:S(2)}, u32[]{:S(2)}) collective-permute-start(bf16[256,256]{1,0:T(8,128)(2,1)S(1)} %get-tuple-element.27), channel_id=1, source_target_pairs={{0,1},{1,0},{2,3},{3,2},{4,5},{5,4},{6,7},{7,6},{8,9},{9,8},{10,11... | collective-permute-start | bytes 393224 | tf_op jit(solution)/shard_map/ppermute | solution.py:346
  45.5 1.0 %collective-permute-done.11 = bf16[256,256]{1,0:T(8,128)(2,1)S(1)} collective-permute-done((bf16[256,256]{1,0:T(8,128)(2,1)S(1)}, bf16[256,256]{1,0:T(8,128)(2,1)S(1)}, u32[]{:S(2)}, u32[]{:S(2)}) %collective-permute-start.11) | collective-permute-done | bytes 131104 | tf_op jit(solution)/shard_map/ppermute | solution.py:346
  46.5 2.5 %collective-permute-start.12 = (bf16[256,256]{1,0:T(8,128)(2,1)S(1)}, bf16[256,256]{1,0:T(8,128)(2,1)S(1)}, u32[]{:S(2)}, u32[]{:S(2)}) collective-permute-start(bf16[256,256]{1,0:T(8,128)(2,1)S(1)} %add_convert_fusion.4), channel_id=1, source_target_pairs={{0,2},{2,0},{4,6},{6,4},{8,10},{10,8},{12,14},{14,12},{1,3},{3,1},... | collective-permute-start | bytes 393224 | tf_op jit(solution)/shard_map/ppermute | solution.py:364
  49.0 1.3 %collective-permute-start.7 = (bf16[2,256,512]{2,1,0:T(8,128)(2,1)S(1)}, bf16[2,256,512]{2,1,0:T(8,128)(2,1)S(1)}, u32[]{:S(2)}, u32[]{:S(2)}) collective-permute-start(bf16[2,256,512]{2,1,0:T(8,128)(2,1)S(1)} %get-tuple-element.23), channel_id=1, source_target_pairs={{1,0},{3,2},{5,4},{7,6},{9,8},{11,10},{13,12},{15,14},{17,16},{19,... | collective-permute-start | bytes 1572872 | tf_op jit(solution)/shard_map/ppermute | solution.py:350
  50.3 2.7 %collective-permute-done.12 = bf16[256,256]{1,0:T(8,128)(2,1)S(1)} collective-permute-done((bf16[256,256]{1,0:T(8,128)(2,1)S(1)}, bf16[256,256]{1,0:T(8,128)(2,1)S(1)}, u32[]{:S(2)}, u32[]{:S(2)}) %collective-permute-start.12) | collective-permute-done | bytes 131104 | tf_op jit(solution)/shard_map/ppermute | solution.py:364
  53.0 1.1 %collective-permute-start.13 = (bf16[256,256]{1,0:T(8,128)(2,1)S(1)}, bf16[256,256]{1,0:T(8,128)(2,1)S(1)}, u32[]{:S(2)}, u32[]{:S(2)}) collective-permute-start(bf16[256,256]{1,0:T(8,128)(2,1)S(1)} %add_convert_fusion.3), channel_id=1, source_target_pairs={{0,4},{2,6},{4,0},{6,2},{8,12},{10,14},{12,8},{14,10},{1,5},{3,7},... | collective-permute-start | bytes 393224 | tf_op jit(solution)/shard_map/ppermute | solution.py:364
  54.1 1.3 %collective-permute-start.9 = (bf16[2,256,512]{2,1,0:T(8,128)(2,1)S(1)}, bf16[2,256,512]{2,1,0:T(8,128)(2,1)S(1)}, u32[]{:S(2)}, u32[]{:S(2)}) collective-permute-start(bf16[2,256,512]{2,1,0:T(8,128)(2,1)S(1)} %get-tuple-element.25), channel_id=1, source_target_pairs={{0,1},{2,3},{4,5},{6,7},{8,9},{10,11},{12,13},{14,15},{16,17},{18,... | collective-permute-start | bytes 1572872 | tf_op jit(solution)/shard_map/ppermute | solution.py:350
  55.4 1.3 %collective-permute-start.5 = (bf16[2,256,512]{2,1,0:T(8,128)(2,1)}, bf16[2,256,512]{2,1,0:T(8,128)(2,1)}, u32[]{:S(2)}, u32[]{:S(2)}) collective-permute-start(bf16[2,256,512]{2,1,0:T(8,128)(2,1)} %get-tuple-element.20), channel_id=1, source_target_pairs={{1,0},{3,2},{5,4},{7,6},{9,8},{11,10},{13,12},{15,14},{17,16},{19,... | collective-permute-start | bytes 1572872 | tf_op jit(solution)/shard_map/ppermute | solution.py:350
  56.7 4.6 %collective-permute-start.6 = (bf16[2,256,512]{2,1,0:T(8,128)(2,1)}, bf16[2,256,512]{2,1,0:T(8,128)(2,1)}, u32[]{:S(2)}, u32[]{:S(2)}) collective-permute-start(bf16[2,256,512]{2,1,0:T(8,128)(2,1)} %get-tuple-element.21), channel_id=1, source_target_pairs={{0,1},{2,3},{4,5},{6,7},{8,9},{10,11},{12,13},{14,15},{16,17},{18,... | collective-permute-start | bytes 1572872 | tf_op jit(solution)/shard_map/ppermute | solution.py:350
  61.3 0.0 collective-permute-done.13
  61.4 0.1 collective-permute-start.14
  61.4 0.0 collective-permute-done.7
  61.5 0.2 add_convert_fusion.1
  61.7 3.3 %collective-permute-start.8 = (bf16[2,256,512]{2,1,0:T(8,128)(2,1)S(1)}, bf16[2,256,512]{2,1,0:T(8,128)(2,1)}, u32[]{:S(2)}, u32[]{:S(2)}) collective-permute-start(bf16[2,256,512]{2,1,0:T(8,128)(2,1)S(1)} %add_convert_fusion.1), channel_id=1, source_target_pairs={{0,2},{2,4},{4,6},{6,8},{8,10},{10,12},{12,14},{16,18},{18,20},{20... | collective-permute-start | bytes 1572872 | tf_op jit(solution)/shard_map/ppermute | solution.py:356
  64.9 0.0 collective-permute-done.9
  65.0 0.2 add_convert_fusion
  65.2 0.7 collective-permute-start.10
  65.9 1.5 %collective-permute-done.14 = bf16[256,256]{1,0:T(8,128)(2,1)S(1)} collective-permute-done((bf16[256,256]{1,0:T(8,128)(2,1)S(1)}, bf16[256,256]{1,0:T(8,128)(2,1)S(1)}, u32[]{:S(2)}, u32[]{:S(2)}) %collective-permute-start.14) | collective-permute-done | bytes 131104 | tf_op jit(solution)/shard_map/ppermute | solution.py:364
  67.4 0.0 copy-done.4
  67.5 0.1 collective-permute-start.15
  67.5 1.5 %collective-permute-done.15 = f32[256,256]{1,0:T(8,128)S(1)} collective-permute-done((f32[256,256]{1,0:T(8,128)S(1)}, f32[256,256]{1,0:T(8,128)S(1)}, u32[]{:S(2)}, u32[]{:S(2)}) %collective-permute-start.15) | collective-permute-done | bytes 262176 | tf_op jit(solution)/shard_map/ppermute | solution.py:346
  69.1 0.8 maximum_select_fusion
  69.9 0.0 collective-permute-done.5
  69.9 0.0 collective-permute-done.6
  69.9 10.9 %collective-permute-done.8 = bf16[2,256,512]{2,1,0:T(8,128)(2,1)} collective-permute-done((bf16[2,256,512]{2,1,0:T(8,128)(2,1)S(1)}, bf16[2,256,512]{2,1,0:T(8,128)(2,1)}, u32[]{:S(2)}, u32[]{:S(2)}) %collective-permute-start.8) | collective-permute-done | bytes 524320 | tf_op jit(solution)/shard_map/ppermute | solution.py:356
  80.8 0.0 collective-permute-done.10
  80.8 3.1 %add_bitcast_fusion = f32[1,2,256,512]{3,2,1,0:T(8,128)} fusion(bf16[2,256,512]{2,1,0:T(8,128)(2,1)S(1)} %collective-permute-done.10, bf16[2,256,512]{2,1,0:T(8,128)(2,1)} %collective-permute-done.8, bf16[2,256,512]{2,1,0:T(8,128)(2,1)} %collective-permute-done.6, bf16[2,256,512]{2,1,0:T(8,128)(2,1)} %collective-permute-done.5, f32[2,256,512]{2,1,0:T(8,128)} %copy-done.4, ...), kind=kLoop, calls=%fused_computation | loop fusion | flops 2359296 | bytes 5242881 | tf_op jit(solution)/shard_map/broadcast_in_dim | solution.py:452
  (17 shorter events, 0.2 us)
Async XLA Ops:
  0.6 12.3 %collective-permute-start.1 = (bf16[2,256,512]{2,1,0:T(8,128)(2,1)}, bf16[2,256,512]{2,1,0:T(8,128)(2,1)S(1)}, u32[]{:S(2)}, u32[]{:S(2)}) collective-permute-start(bf16[2,256,512]{2,1,0:T(8,128)(2,1)} %bitcast.5.own_ref), channel_id=1, source_target_pairs={{2,0},{4,2},{6,4},{8,6},{10,8},{12,10},{14,12},{18,16},{20,18},{22... | collective-permute-start | bytes 1572872 | tf_op jit(solution)/shard_map/ppermute | solution.py:356
  4.0 1.2 %copy-start.9 = (bf16[1,8,1,256,256]{4,3,2,1,0:T(8,128)(2,1)S(1)}, bf16[1,8,1,256,256]{4,3,2,1,0:T(8,128)(2,1)}, u32[]{:S(2)}) copy-start(bf16[1,8,1,256,256]{4,3,2,1,0:T(8,128)(2,1)} %param.11) | copy-start | bytes 3145732
  5.2 0.9 %copy-start.15 = (bf16[256,256]{1,0:T(8,128)(2,1)S(1)}, bf16[256,256]{1,0:T(8,128)(2,1)}, u32[]{:S(2)}) copy-start(bf16[256,256]{1,0:T(8,128)(2,1)} %constant.37.clone.perm_ref) | copy-start | bytes 393220
  6.1 19.0 %copy-start.1 = (bf16[4,320,256]{2,1,0:T(8,128)(2,1)S(1)}, bf16[4,320,256]{2,1,0:T(8,128)(2,1)}, u32[]{:S(2)}) copy-start(bf16[4,320,256]{2,1,0:T(8,128)(2,1)} %constant.35.clone.prop_ref) | copy-start | bytes 1966084
  8.0 1.0 %copy-start.16 = (bf16[8,256,256]{2,1,0:T(8,128)(2,1)}, bf16[8,256,256]{2,1,0:T(8,128)(2,1)S(1)}, u32[]{:S(2)}) copy-start(bf16[8,256,256]{2,1,0:T(8,128)(2,1)S(1)} %get-tuple-element.16.meas_ref) | copy-start | bytes 3145732
  9.0 16.1 %copy-start.6 = (s32[1,8,1]{1,2,0:T(1,128)S(1)}, s32[1,8,1]{1,2,0:T(1,128)}, u32[]{:S(2)}) copy-start(s32[1,8,1]{1,2,0:T(1,128)} %param.12) | copy-start | bytes 100
  9.0 16.1 %copy-start.8 = (s32[1,8,1]{1,2,0:T(1,128)S(1)}, s32[1,8,1]{1,2,0:T(1,128)}, u32[]{:S(2)}) copy-start(s32[1,8,1]{1,2,0:T(1,128)} %param.13) | copy-start | bytes 100
  9.0 5.2 %collective-permute-start.3 = (bf16[2,256,512]{2,1,0:T(8,128)(2,1)S(1)}, bf16[2,256,512]{2,1,0:T(8,128)(2,1)S(1)}, u32[]{:S(2)}, u32[]{:S(2)}) collective-permute-start(bf16[2,256,512]{2,1,0:T(8,128)(2,1)S(1)} %get-tuple-element.15), channel_id=1, source_target_pairs={{3,1},{5,3},{7,5},{9,7},{11,9},{13,11},{15,13},{19,17},{21,19},{23... | collective-permute-start | bytes 1572872 | tf_op jit(solution)/shard_map/ppermute | solution.py:356
  9.8 6.5 %collective-permute-start = (bf16[2,256,512]{2,1,0:T(8,128)(2,1)}, bf16[2,256,512]{2,1,0:T(8,128)(2,1)S(1)}, u32[]{:S(2)}, u32[]{:S(2)}) collective-permute-start(bf16[2,256,512]{2,1,0:T(8,128)(2,1)} %bitcast.5.own_ref), channel_id=1, source_target_pairs={{0,1},{1,0},{2,3},{3,2},{4,5},{5,4},{6,7},{7,6},{8,9},{9,8},{10,11... | collective-permute-start | bytes 1572872 | tf_op jit(solution)/shard_map/ppermute | solution.py:346
  12.9 3.4 %collective-permute-start.2 = (bf16[2,256,512]{2,1,0:T(8,128)(2,1)S(1)}, bf16[2,256,512]{2,1,0:T(8,128)(2,1)S(1)}, u32[]{:S(2)}, u32[]{:S(2)}) collective-permute-start(bf16[2,256,512]{2,1,0:T(8,128)(2,1)S(1)} %collective-permute-done.1.halo_ref), channel_id=1, source_target_pairs={{0,1},{2,3},{4,5},{6,7},{8,9},{10,11},{12,13},{14,15},{16,17},{18,... | collective-permute-start | bytes 1572872 | tf_op jit(solution)/shard_map/ppermute | solution.py:350
  14.3 10.1 %copy-start.10 = (bf16[2,256,512]{2,1,0:T(8,128)(2,1)}, bf16[2,256,512]{2,1,0:T(8,128)(2,1)S(1)}, u32[]{:S(2)}) copy-start(bf16[2,256,512]{2,1,0:T(8,128)(2,1)S(1)} %collective-permute-done.3.halo_ref) | copy-start | bytes 1572868
  14.3 10.0 %collective-permute-start.4 = (bf16[2,256,512]{2,1,0:T(8,128)(2,1)S(1)}, bf16[2,256,512]{2,1,0:T(8,128)(2,1)S(1)}, u32[]{:S(2)}, u32[]{:S(2)}) collective-permute-start(bf16[2,256,512]{2,1,0:T(8,128)(2,1)S(1)} %collective-permute-done.3.halo_ref), channel_id=1, source_target_pairs={{1,0},{3,2},{5,4},{7,6},{9,8},{11,10},{13,12},{15,14},{17,16},{19,... | collective-permute-start | bytes 1572872 | tf_op jit(solution)/shard_map/ppermute | solution.py:350
  16.3 1.1 %copy-start = (bf16[4,320,256]{2,1,0:T(8,128)(2,1)S(1)}, bf16[4,320,256]{2,1,0:T(8,128)(2,1)}, u32[]{:S(2)}) copy-start(bf16[4,320,256]{2,1,0:T(8,128)(2,1)} %constant.35.clone.prop_ref) | copy-start | bytes 1966084
  17.4 0.9 %copy-start.2 = (bf16[2,256,256]{2,1,0:T(8,128)(2,1)S(1)}, bf16[2,256,256]{2,1,0:T(8,128)(2,1)}, u32[]{:S(2)}) copy-start(bf16[2,256,256]{2,1,0:T(8,128)(2,1)} %probe_ref.3) | copy-start | bytes 786436
  18.4 0.7 copy-start.5
  19.0 0.7 copy-start.7
  19.7 5.5 %copy-start.14 = (bf16[4,256,256]{2,1,0:T(8,128)(2,1)S(1)}, bf16[4,256,256]{2,1,0:T(8,128)(2,1)}, u32[]{:S(2)}) copy-start(bf16[4,256,256]{2,1,0:T(8,128)(2,1)} %constant.36.clone.four_ref) | copy-start | bytes 1572868
  19.7 5.5 %copy-start.17 = (bf16[8,256,256]{2,1,0:T(8,128)(2,1)S(1)}, bf16[8,256,256]{2,1,0:T(8,128)(2,1)}, u32[]{:S(2)}) copy-start(bf16[8,256,256]{2,1,0:T(8,128)(2,1)} %copy-done.16) | copy-start | bytes 3145732
  24.3 0.8 copy-start.12
  25.1 1.0 %copy-start.11 = (bf16[2,256,512]{2,1,0:T(8,128)(2,1)S(1)}, bf16[2,256,512]{2,1,0:T(8,128)(2,1)}, u32[]{:S(2)}) copy-start(bf16[2,256,512]{2,1,0:T(8,128)(2,1)} %copy-done.10) | copy-start | bytes 1572868
  26.2 1.0 %copy-start.13 = (bf16[2,256,512]{2,1,0:T(8,128)(2,1)S(1)}, bf16[2,256,512]{2,1,0:T(8,128)(2,1)}, u32[]{:S(2)}) copy-start(bf16[2,256,512]{2,1,0:T(8,128)(2,1)} %copy-done.12) | copy-start | bytes 1572868
  27.2 8.6 %copy-start.3 = (bf16[2,256,256]{2,1,0:T(8,128)(2,1)S(1)}, bf16[2,256,256]{2,1,0:T(8,128)(2,1)}, u32[]{:S(2)}) copy-start(bf16[2,256,256]{2,1,0:T(8,128)(2,1)} %probe_ref.3) | copy-start | bytes 786436
  42.5 24.9 %copy-start.4 = (f32[2,256,512]{2,1,0:T(8,128)}, f32[2,256,512]{2,1,0:T(8,128)S(1)}, u32[]{:S(2)}) copy-start(f32[2,256,512]{2,1,0:T(8,128)S(1)} %get-tuple-element.18) | copy-start | bytes 3145732
  42.5 3.9 %collective-permute-start.11 = (bf16[256,256]{1,0:T(8,128)(2,1)S(1)}, bf16[256,256]{1,0:T(8,128)(2,1)S(1)}, u32[]{:S(2)}, u32[]{:S(2)}) collective-permute-start(bf16[256,256]{1,0:T(8,128)(2,1)S(1)} %get-tuple-element.27), channel_id=1, source_target_pairs={{0,1},{1,0},{2,3},{3,2},{4,5},{5,4},{6,7},{7,6},{8,9},{9,8},{10,11... | collective-permute-start | bytes 393224 | tf_op jit(solution)/shard_map/ppermute | solution.py:346
  46.5 6.5 %collective-permute-start.12 = (bf16[256,256]{1,0:T(8,128)(2,1)S(1)}, bf16[256,256]{1,0:T(8,128)(2,1)S(1)}, u32[]{:S(2)}, u32[]{:S(2)}) collective-permute-start(bf16[256,256]{1,0:T(8,128)(2,1)S(1)} %add_convert_fusion.4), channel_id=1, source_target_pairs={{0,2},{2,0},{4,6},{6,4},{8,10},{10,8},{12,14},{14,12},{1,3},{3,1},... | collective-permute-start | bytes 393224 | tf_op jit(solution)/shard_map/ppermute | solution.py:364
  49.0 12.5 %collective-permute-start.7 = (bf16[2,256,512]{2,1,0:T(8,128)(2,1)S(1)}, bf16[2,256,512]{2,1,0:T(8,128)(2,1)S(1)}, u32[]{:S(2)}, u32[]{:S(2)}) collective-permute-start(bf16[2,256,512]{2,1,0:T(8,128)(2,1)S(1)} %get-tuple-element.23), channel_id=1, source_target_pairs={{1,0},{3,2},{5,4},{7,6},{9,8},{11,10},{13,12},{15,14},{17,16},{19,... | collective-permute-start | bytes 1572872 | tf_op jit(solution)/shard_map/ppermute | solution.py:350
  53.0 8.3 %collective-permute-start.13 = (bf16[256,256]{1,0:T(8,128)(2,1)S(1)}, bf16[256,256]{1,0:T(8,128)(2,1)S(1)}, u32[]{:S(2)}, u32[]{:S(2)}) collective-permute-start(bf16[256,256]{1,0:T(8,128)(2,1)S(1)} %add_convert_fusion.3), channel_id=1, source_target_pairs={{0,4},{2,6},{4,0},{6,2},{8,12},{10,14},{12,8},{14,10},{1,5},{3,7},... | collective-permute-start | bytes 393224 | tf_op jit(solution)/shard_map/ppermute | solution.py:364
  54.1 10.8 %collective-permute-start.9 = (bf16[2,256,512]{2,1,0:T(8,128)(2,1)S(1)}, bf16[2,256,512]{2,1,0:T(8,128)(2,1)S(1)}, u32[]{:S(2)}, u32[]{:S(2)}) collective-permute-start(bf16[2,256,512]{2,1,0:T(8,128)(2,1)S(1)} %get-tuple-element.25), channel_id=1, source_target_pairs={{0,1},{2,3},{4,5},{6,7},{8,9},{10,11},{12,13},{14,15},{16,17},{18,... | collective-permute-start | bytes 1572872 | tf_op jit(solution)/shard_map/ppermute | solution.py:350
  55.4 14.5 %collective-permute-start.5 = (bf16[2,256,512]{2,1,0:T(8,128)(2,1)}, bf16[2,256,512]{2,1,0:T(8,128)(2,1)}, u32[]{:S(2)}, u32[]{:S(2)}) collective-permute-start(bf16[2,256,512]{2,1,0:T(8,128)(2,1)} %get-tuple-element.20), channel_id=1, source_target_pairs={{1,0},{3,2},{5,4},{7,6},{9,8},{11,10},{13,12},{15,14},{17,16},{19,... | collective-permute-start | bytes 1572872 | tf_op jit(solution)/shard_map/ppermute | solution.py:350
  56.7 13.2 %collective-permute-start.6 = (bf16[2,256,512]{2,1,0:T(8,128)(2,1)}, bf16[2,256,512]{2,1,0:T(8,128)(2,1)}, u32[]{:S(2)}, u32[]{:S(2)}) collective-permute-start(bf16[2,256,512]{2,1,0:T(8,128)(2,1)} %get-tuple-element.21), channel_id=1, source_target_pairs={{0,1},{2,3},{4,5},{6,7},{8,9},{10,11},{12,13},{14,15},{16,17},{18,... | collective-permute-start | bytes 1572872 | tf_op jit(solution)/shard_map/ppermute | solution.py:350
  61.4 6.0 %collective-permute-start.14 = (bf16[256,256]{1,0:T(8,128)(2,1)S(1)}, bf16[256,256]{1,0:T(8,128)(2,1)S(1)}, u32[]{:S(2)}, u32[]{:S(2)}) collective-permute-start(bf16[256,256]{1,0:T(8,128)(2,1)S(1)} %add_convert_fusion.2), channel_id=1, source_target_pairs={{0,8},{2,10},{4,12},{6,14},{8,0},{10,2},{12,4},{14,6},{1,9},{3,11}... | collective-permute-start | bytes 393224 | tf_op jit(solution)/shard_map/ppermute | solution.py:364
  61.7 19.2 %collective-permute-start.8 = (bf16[2,256,512]{2,1,0:T(8,128)(2,1)S(1)}, bf16[2,256,512]{2,1,0:T(8,128)(2,1)}, u32[]{:S(2)}, u32[]{:S(2)}) collective-permute-start(bf16[2,256,512]{2,1,0:T(8,128)(2,1)S(1)} %add_convert_fusion.1), channel_id=1, source_target_pairs={{0,2},{2,4},{4,6},{6,8},{8,10},{10,12},{12,14},{16,18},{18,20},{20... | collective-permute-start | bytes 1572872 | tf_op jit(solution)/shard_map/ppermute | solution.py:356
  65.2 15.7 %collective-permute-start.10 = (bf16[2,256,512]{2,1,0:T(8,128)(2,1)S(1)}, bf16[2,256,512]{2,1,0:T(8,128)(2,1)S(1)}, u32[]{:S(2)}, u32[]{:S(2)}) collective-permute-start(bf16[2,256,512]{2,1,0:T(8,128)(2,1)S(1)} %add_convert_fusion), channel_id=1, source_target_pairs={{1,3},{3,5},{5,7},{7,9},{9,11},{11,13},{13,15},{17,19},{19,21},{21... | collective-permute-start | bytes 1572872 | tf_op jit(solution)/shard_map/ppermute | solution.py:356
  67.5 1.6 %collective-permute-start.15 = (f32[256,256]{1,0:T(8,128)S(1)}, f32[256,256]{1,0:T(8,128)S(1)}, u32[]{:S(2)}, u32[]{:S(2)}) collective-permute-start(f32[256,256]{1,0:T(8,128)S(1)} %get-tuple-element.29), channel_id=1, source_target_pairs={{0,1},{1,0},{2,3},{3,2},{4,5},{5,4},{6,7},{7,6},{8,9},{9,8},{10,11... | collective-permute-start | bytes 786440 | tf_op jit(solution)/shard_map/ppermute | solution.py:346

commit v3 on v2

v3 whole, which is shorter than its diff:
```python
import functools
import math

import jax
import jax.numpy as jnp
import ml_dtypes
import numpy as np
from jax import lax
from jax.experimental import pallas as pl
from jax.experimental.pallas import tpu as pltpu
from jax.sharding import PartitionSpec as P

BAND = 32
LANES = 128
CHUNK = 16
WIN_CHUNK = 32
GROUP = 4
MIB = 1024 * 1024
f32 = jnp.float32
bf16 = jnp.bfloat16


def tables(size):
    index = np.arange(size, dtype=np.int32)
    offset = index[:, None] - index[None, :]
    inside = (np.abs(offset) <= BAND).astype(np.float32)
    offset_f = offset.astype(np.float32)
    phase = (np.float32(math.pi) * offset_f * offset_f / np.float32(2.0 * BAND)).astype(np.float32)
    scale = np.float32(1.0 / math.sqrt(2 * BAND + 1))
    prop_re = np.cos(phase) * inside * scale
    prop_im = np.sin(phase) * inside * scale
    product = (index[:, None] * index[None, :]) % size
    angle = (np.float32(-2.0 * math.pi) * product.astype(np.float32) / np.float32(size)).astype(np.float32)
    root = np.float32(math.sqrt(size))
    return prop_re, prop_im, np.cos(angle) / root, np.sin(angle) / root


def packed(mat_re, mat_im):
    n, k = mat_re.shape
    upper = np.concatenate([mat_re, -mat_im], axis=1).reshape(n // CHUNK, 1, CHUNK, 2 * k)
    lower = np.concatenate([mat_im, mat_re], axis=1).reshape(n // CHUNK, 1, CHUNK, 2 * k)
    both = np.concatenate([upper, lower], axis=1).reshape(2 * n, 2 * k)
    return both.astype(np.float32).astype(ml_dtypes.bfloat16)


def constants(size):
    half = size // 2
    kr, ki, fr, fi = tables(size)
    near, far = half + BAND, half - BAND
    prop = [
        packed(kr[:near, :half], ki[:near, :half]),
        packed(kr[far:, half:], ki[far:, half:]),
        packed(kr[:near, :half], -ki[:near, :half]),
        packed(kr[far:, half:], -ki[far:, half:]),
    ]
    four = [
        packed(fr[0::2, :half], fi[0::2, :half]),
        packed(fr[1::2, :half], fi[1::2, :half]),
        packed(fr[:half, 0::2], -fi[:half, 0::2]),
        packed(fr[:half, 1::2], -fi[:half, 1::2]),
    ]
    order = np.concatenate([np.arange(0, size, 2), np.arange(1, size, 2)])
    perm = np.eye(size, dtype=np.float32)[order].astype(ml_dtypes.bfloat16)
    return np.stack(prop), np.stack(four), perm


def nt(left, right):
    return lax.dot_general(left, right, (((1,), (1,)), ((), ())), preferred_element_type=f32)


def banded(prop_ref, base, source):
    size = source.shape[1] // 2
    skip = (size // 2 - BAND) // CHUNK
    stop = (size // 2 + BAND) // CHUNK
    first = nt(prop_ref[base], source[:, :size])
    second = nt(prop_ref[base + 1], source[:, size:])

    def at(j):
        out = []
        for part in range(2):
            value = None
            if j < stop:
                lo = (2 * j + part) * CHUNK
                value = first[lo : lo + CHUNK]
            if j >= skip:
                lo = (2 * (j - skip) + part) * CHUNK
                more = second[lo : lo + CHUNK]
                value = more if value is None else value + more
            out.append(value)
        return out

    return at


def halves(four_ref, base, source):
    size = source.shape[1] // 2
    first = nt(four_ref[base], source[:, :size])
    second = nt(four_ref[base + 1], source[:, size:])

    def at(j):
        lo = 2 * j * CHUNK
        return (
            (first[lo : lo + CHUNK], first[lo + CHUNK : lo + 2 * CHUNK]),
            (second[lo : lo + CHUNK], second[lo + CHUNK : lo + 2 * CHUNK]),
        )

    return at


def put(target, lo, re, im):
    half = re.shape[1] // 2
    target[lo : lo + CHUNK, :] = jnp.concatenate(
        [re[:, :half], im[:, :half], re[:, half:], im[:, half:]], axis=1
    ).astype(bf16)


def put_butterfly(target, lo, re, im):
    half = re.shape[1] // 2
    target[lo : lo + CHUNK, :] = jnp.concatenate(
        [
            re[:, :half] + re[:, half:],
            im[:, :half] + im[:, half:],
            re[:, :half] - re[:, half:],
            im[:, :half] - im[:, half:],
        ],
        axis=1,
    ).astype(bf16)


class Place:
    def __init__(self, row, col):
        self.row = row
        self.block = lax.shift_right_logical(col, 7)
        self.shift = jnp.bitwise_and(col, LANES - 1)


def fill(ext, core, strips, halos):
    strip = strips[0].shape[1]
    for side in range(2):

        @pl.when(core == side)
        def _():
            for part in range(2):
                for block in range(strips[side].shape[2] // LANES):
                    lanes = slice(block * LANES, (block + 1) * LANES)
                    ext[part, block, :strip, :] = strips[side][part, :, lanes].astype(f32)
                    ext[part, block, strip:, :] = halos[side][part, :, lanes].astype(f32)


def window(ext, win, place):
    size = win.shape[1]
    back = jnp.bitwise_and(LANES - place.shift, LANES - 1)
    keep = lax.broadcasted_iota(jnp.int32, (WIN_CHUNK, LANES), 1) < LANES - place.shift
    for lo in range(0, size, WIN_CHUNK):
        span = slice(lo, lo + WIN_CHUNK)
        for part in range(2):
            loaded = [
                pltpu.roll(ext[part, place.block + i, pl.ds(place.row + lo, WIN_CHUNK), :], back, 1)
                for i in range(3)
            ]
            win[part, span, :LANES] = jnp.where(keep, loaded[0], loaded[1])
            win[part, span, LANES:] = jnp.where(keep, loaded[1], loaded[2])


def scatter(acc, place, lo, parts):
    low = lax.broadcasted_iota(jnp.int32, (CHUNK, LANES), 1) < place.shift
    for part, value in enumerate(parts):
        left = pltpu.roll(value[:, :LANES], place.shift, 1)
        right = pltpu.roll(value[:, LANES:], place.shift, 1)
        pieces = (jnp.where(low, 0.0, left), jnp.where(low, left, right), jnp.where(low, right, 0.0))
        for i, piece in enumerate(pieces):
            at = (part, place.block + i, pl.ds(place.row + lo, CHUNK), slice(None))
            acc[at] = acc[at] + piece


def members(step, live):
    for g in range(GROUP):
        slot = step * GROUP + g
        yield jnp.minimum(slot, live - 1), slot < live


def place_of(info_ref, slots, slot):
    return Place(info_ref[2 + slot], info_ref[2 + slots + slot])


def pass_kernel(after_ref, value_ref, out_ref):
    pass


def prepare_kernel(info_ref, meas_ref, perm_ref, probe_ref, prop_ref, four_ref, out_ref):
    perm = perm_ref[...]
    for slot in range(meas_ref.shape[0]):
        rows = jnp.dot(perm, meas_ref[slot], preferred_element_type=f32).astype(bf16)
        out_ref[slot] = nt(rows, perm).astype(bf16)


def positions_kernel(
    info_ref, own_ref, other_ref, halo_own_ref, halo_other_ref, meas_ref, probe_ref, prop_ref, four_ref,
    grads_ref, mine_ref, theirs_ref,
    ext_a, ext_b, win_a, win_b, wave, x_a, x_b, pro, pacc,
):
    size = meas_ref.shape[1]
    half = size // 2
    steps = size // CHUNK
    core, live = info_ref[0], info_ref[1]
    slots = meas_ref.shape[0]
    fill(ext_a, core, (own_ref, other_ref), (halo_own_ref, halo_other_ref))
    fill(ext_b, core, (other_ref, own_ref), (halo_other_ref, halo_own_ref))
    pacc[...] = jnp.zeros(pacc.shape, f32)
    pro[...] = probe_ref[...].astype(f32)

    def visit(step, _):
        group = list(members(step, live))
        for g, (slot, _) in enumerate(group):
            place = place_of(info_ref, slots, slot)
            window(ext_a, win_a.at[g], place)
            window(ext_b, win_b.at[g], place)
            for j in range(steps):
                span = slice(j * CHUNK, (j + 1) * CHUNK)
                pr, pi = pro[0, span], pro[1, span]
                wr, wi = win_a[g, 0, span], win_a[g, 1, span]
                put(x_a.at[g], j * CHUNK, pr * wr - pi * wi, pr * wi + pi * wr)
        for g in range(GROUP):
            at = banded(prop_ref, 0, x_a[g])
            for j in range(steps):
                put(x_b.at[g], j * CHUNK, *at(j))
        for g in range(GROUP):
            at = banded(prop_ref, 0, x_b[g])
            for j in range(steps):
                span = slice(j * CHUNK, (j + 1) * CHUNK)
                re, im = at(j)
                wave[g, 0, span] = re
                wave[g, 1, span] = im
                wr, wi = win_b[g, 0, span], win_b[g, 1, span]
                put_butterfly(x_a.at[g], j * CHUNK, re * wr - im * wi, re * wi + im * wr)
        for g in range(GROUP):
            at = halves(four_ref, 0, x_a[g])
            for j in range(steps // 2):
                even, odd = at(j)
                put_butterfly(x_b.at[g], j * CHUNK, *even)
                put_butterfly(x_b.at[g], half + j * CHUNK, *odd)
        for g, (slot, _) in enumerate(group):
            at = halves(four_ref, 0, x_b[g])
            for j in range(steps // 2):
                for side, (re, im) in enumerate(at(j)):
                    lo = side * half + j * CHUNK
                    misfit = re * re + im * im - meas_ref[slot, lo : lo + CHUNK, :].astype(f32)
                    put(x_a.at[g], lo, misfit * re, misfit * im)
        for g in range(GROUP):
            at = halves(four_ref, 2, x_a[g])
            for j in range(steps // 2):
                (er, ei), (dr, di) = at(j)
                put(x_b.at[g], j * CHUNK, er + dr, ei + di)
                put(x_b.at[g], half + j * CHUNK, er - dr, ei - di)
        for g, (slot, _) in enumerate(group):
            at = halves(four_ref, 2, x_b[g])
            for j in range(steps // 2):
                (er, ei), (dr, di) = at(j)
                for side in range(2):
                    lo = side * half + j * CHUNK
                    span = slice(lo, lo + CHUNK)
                    re, im = (er + dr, ei + di) if side == 0 else (er - dr, ei - di)
                    br, bi = wave[g, 0, span], wave[g, 1, span]
                    wr, wi = win_b[g, 0, span], win_b[g, 1, span]
                    grads_ref[1, slot, 0, span] = (re * br + im * bi).astype(bf16)
                    grads_ref[1, slot, 1, span] = (im * br - re * bi).astype(bf16)
                    put(x_a.at[g], lo, re * wr + im * wi, im * wr - re * wi)
        for g in range(GROUP):
            at = banded(prop_ref, 2, x_a[g])
            for j in range(steps):
                put(x_b.at[g], j * CHUNK, *at(j))
        for g, (slot, valid) in enumerate(group):
            at = banded(prop_ref, 2, x_b[g])
            for j in range(steps):
                span = slice(j * CHUNK, (j + 1) * CHUNK)
                re, im = at(j)
                pr, pi = pro[0, span], pro[1, span]
                grads_ref[0, slot, 0, span] = (re * pr + im * pi).astype(bf16)
                grads_ref[0, slot, 1, span] = (im * pr - re * pi).astype(bf16)
                wr, wi = win_a[g, 0, span], win_a[g, 1, span]
                pacc[0, span] = pacc[0, span] + jnp.where(valid, re * wr + im * wi, 0.0)
                pacc[1, span] = pacc[1, span] + jnp.where(valid, im * wr - re * wi, 0.0)
        return 0

    lax.fori_loop(0, (live + GROUP - 1) // GROUP, visit, 0)
    mine_ref[...] = pacc[core]
    theirs_ref[...] = pacc[1 - core].astype(bf16)


def placing_kernel(own_slice, info_ref, grads_ref, after_ref, strip_ref, tail_ref, token_ref, acc):
    strip, ny = strip_ref.shape[1:]
    slots = grads_ref.shape[1]
    core, live = info_ref[0], info_ref[1]
    which = core if own_slice else 1 - core
    acc[...] = jnp.zeros(acc.shape, f32)

    def visit(slot, _):
        place = place_of(info_ref, slots, slot)
        for lo in range(0, grads_ref.shape[3], CHUNK):
            parts = [grads_ref[which, slot, part, lo : lo + CHUNK, :].astype(f32) for part in range(2)]
            scatter(acc, place, lo, parts)
        return 0

    lax.fori_loop(0, live, visit, 0)
    for part in range(2):
        for block in range(ny // LANES):
            lanes = slice(block * LANES, (block + 1) * LANES)
            strip_ref[part, :, lanes] = acc[part, block, :strip, :].astype(strip_ref.dtype)
            tail_ref[part, :, lanes] = acc[part, block, strip:, :].astype(tail_ref.dtype)
    token_ref[...] = jnp.zeros(token_ref.shape, token_ref.dtype)


def swap(value):
    return lax.ppermute(value, "pos", [(0, 1), (1, 0)])


def shift_tile(value, by):
    peers = lax.axis_size("tile")
    return lax.ppermute(value, "tile", [(i, i + by) for i in range(peers) if 0 <= i + by < peers])


def call(mib, body, results, operands, info, scratch, loose=(), alias=None):
    vmem = pl.BlockSpec(memory_space=pltpu.VMEM)
    smem = pl.BlockSpec(memory_space=pltpu.SMEM)
    spots = [smem] * len(info) + [pl.BlockSpec(memory_space=pl.ANY) if i in loose else vmem for i in range(len(operands))]
    return pl.pallas_call(
        body,
        out_shape=tuple(results),
        in_specs=spots,
        out_specs=(pl.BlockSpec(memory_space=pl.ANY) if alias else vmem,) * len(results),
        scratch_shapes=scratch,
        input_output_aliases=alias or {},
        cost_estimate=pl.CostEstimate(flops=2**20, bytes_accessed=2**12, transcendentals=0),
        compiler_params=pltpu.CompilerParams(vmem_limit_bytes=mib * MIB),
    )(*info, *operands)


def local(object_slices, probe, intensity, scan_rows, scan_cols, counts):
    strip, ny = object_slices.shape[2:]
    size = probe.shape[1]
    slots = intensity.shape[1]
    cores = lax.axis_size("pos")
    core = lax.axis_index("pos")
    peers = lax.axis_size("tile")
    prop, four, perm = (jnp.asarray(t) for t in constants(size))
    sds = jax.ShapeDtypeStruct
    own = object_slices[0]
    live = jnp.minimum(jnp.maximum(counts[0, 0] - core + cores - 1, 0) // cores, slots)
    info = (jnp.concatenate([jnp.stack([core, live]).astype(jnp.int32), scan_rows.reshape(-1), scan_cols.reshape(-1)]),)
    blocks = ny // LANES + 1

    halo_own = shift_tile(own, -1)
    other = swap(own)
    (measured,) = call(
        12,
        prepare_kernel,
        (sds((slots, size, size), bf16),),
        (intensity.reshape(slots, size, size), perm, probe, prop, four),
        info, [],
    )
    (halo_own,) = call(4, pass_kernel, (sds(halo_own.shape, bf16),), (measured, halo_own), (), [], loose=(0, 1), alias={1: 0})
    halo_other = swap(halo_own)

    ext = pltpu.VMEM((2, blocks, 2 * strip, LANES), f32)
    win = pltpu.VMEM((GROUP, 2, size, size), f32)
    half_wave = pltpu.VMEM((GROUP, size, 2 * size), bf16)
    full = pltpu.VMEM((2, size, size), f32)
    grads, mine, theirs = call(
        30,
        positions_kernel,
        (sds((2, slots, 2, size, size), bf16), sds((size, size), f32), sds((size, size), bf16)),
        (own, other, halo_own, halo_other, measured, probe, prop, four),
        info, [ext, ext, win, win, win, half_wave, half_wave, full, full],
    )
    rows = (2, strip, ny)
    flat = sds((size, size), bf16)
    away_strip, away_tail, token = call(
        12,
        functools.partial(placing_kernel, False),
        (sds(rows, bf16), sds(rows, bf16), flat), (grads, grads), info, [ext], loose=(1,),
    )
    part = mine + swap(theirs).astype(f32)
    part = part.astype(bf16)
    own_strip, own_tail, token = call(
        12,
        functools.partial(placing_kernel, True),
        (sds(rows, f32), sds(rows, bf16), flat), (grads, part), info, [ext], loose=(1,),
    )
    above = shift_tile((own_tail.astype(f32) + swap(away_tail).astype(f32)).astype(bf16), 1)
    step = 1
    while step < peers:
        got = lax.ppermute(part, "tile", [(i, i ^ step) for i in range(peers)])
        if 2 * step >= peers:
            (got,) = call(4, pass_kernel, (sds(got.shape, bf16),), (above, got), (), [], loose=(0, 1), alias={1: 0})
        total = part.astype(f32) + got.astype(f32)
        if step == 1:
            total = total + token.astype(f32)
        part = total.astype(bf16)
        step *= 2

    owned = lax.optimization_barrier(own_strip + swap(away_strip).astype(f32))
    owned = owned + above.astype(f32)

    part = total / math.sqrt(peers * slots * cores)
    again = swap(part)
    probe_total = jnp.where(core == 0, jnp.stack([part, again]), jnp.stack([again, part]))
    return owned[None], probe_total


def solution(mesh):
    placed = (
        P("pos", "grp", "tile", None),
        P("grp", None, None),
        P("tile", "grp", "pos", None, None),
        P("tile", "grp", "pos"),
        P("tile", "grp", "pos"),
        P("grp", "tile"),
    )
    return jax.shard_map(
        local,
        mesh=mesh,
        in_specs=placed,
        out_specs=(P("pos", "grp", "tile", None), P("grp", None, None)),
        check_vma=False,
    )
```

time: 84.7 us -> 62.3 us (0.74)
  the two profiles are of different devices: /device:TPU:16 before, /device:TPU:29 now
where the time goes in v3:
time: 62.3 us; the launch traced here: 62.5 us
  waiting for transfers between devices  21.9 us (35%)
  starting transfers between devices  18.9 us (30%)
  Pallas kernels  9.62 us (15%)
  local copies, waits for them, and re-layouts  7.41 us (12%)
  other arithmetic  3.2 us (5%)
  between operations  1.41 us (2%)
    ppermute x3, waiting for transfers between devices, local(): got = lax.ppermute(part, 'tile', [(i, i ^ step) for i in range(peers)])  18.5 us
    pallas_call x6, Pallas kernels, call(): pl.pallas_call(body, out_shape=tuple(results), in_specs=spots, out_specs=...  9.62 us
    ppermute x3, starting transfers between devices, local(): got = lax.ppermute(part, 'tile', [(i, i ^ step) for i in range(peers)])  8.72 us
    unnamed x20, local copies, waits for them, and re-layouts  7.41 us
    ppermute x6, starting transfers between devices, swap(): return lax.ppermute(value, 'pos', [(0, 1), (1, 0)])  6.76 us
    ppermute x2, starting transfers between devices, shift_tile(): lax.ppermute(value, 'tile', [(i, i + by) for i in range(peers) if 0 <= i...  3.46 us
    ppermute x2, waiting for transfers between devices, shift_tile(): lax.ppermute(value, 'tile', [(i, i + by) for i in range(peers) if 0 <= i...  1.85 us
    ppermute x6, waiting for transfers between devices, swap(): return lax.ppermute(value, 'pos', [(0, 1), (1, 0)])  1.56 us
  transfers between devices with their start and end apart: 11, of which 4 were waited for; matrix products, arithmetic and copies ran while one was open for 4% of the time, Pallas kernels for 6%

profile of v3, /device:TPU:29, one launch (start us, length us, event | category | flops | bytes accessed | tf_op | source)
XLA Modules:
  0.0 62.5 jit_solution(12054259083337443772)
XLA Ops:
  0.6 2.2 %collective-permute-start.1 = (bf16[2,256,512]{2,1,0:T(8,128)(2,1)}, bf16[2,256,512]{2,1,0:T(8,128)(2,1)S(1)}, u32[]{:S(2)}, u32[]{:S(2)}) collective-permute-start(bf16[2,256,512]{2,1,0:T(8,128)(2,1)} %bitcast.14), channel_id=1, source_target_pairs={{2,0},{4,2},{6,4},{8,6},{10,8},{12,10},{14,12},{3,1},{5,3},{7,5},{... | collective-permute-start | bytes 1572872 | tf_op jit(solution)/shard_map/ppermute | solution.py:319
  2.8 1.0 %collective-permute-start = (bf16[2,256,512]{2,1,0:T(8,128)(2,1)}, bf16[2,256,512]{2,1,0:T(8,128)(2,1)S(1)}, u32[]{:S(2)}, u32[]{:S(2)}) collective-permute-start(bf16[2,256,512]{2,1,0:T(8,128)(2,1)} %bitcast.15), channel_id=1, source_target_pairs={{0,1},{1,0},{2,3},{3,2},{4,5},{5,4},{6,7},{7,6},{8,9},{9,8},{10,11... | collective-permute-start | bytes 1572872 | tf_op jit(solution)/shard_map/ppermute | solution.py:314
  4.5 0.8 %pad_add_fusion.info_ref = s32[18]{0:T(128)S(1)} fusion(s32[8]{0:T(128)} %bitcast.18, s32[8]{0:T(128)} %bitcast.19, s32[1]{0:T(128)} %bitcast.2, s32[1]{0:T(128)} %bitcast), kind=kLoop, calls=%fused_computation.8 | loop fusion | flops 54 | bytes 144 | tf_op jit(solution)/shard_map/concatenate | solution.py:349
  5.2 0.0 copy-start.2
  5.2 1.1 %copy-done.2 = bf16[4,320,256]{2,1,0:T(8,128)(2,1)S(1)} copy-done((bf16[4,320,256]{2,1,0:T(8,128)(2,1)S(1)}, bf16[4,320,256]{2,1,0:T(8,128)(2,1)}, u32[]{:S(2)}) %copy-start.2) | copy-done | bytes 655384
  6.3 0.0 copy-start.4
  6.3 1.0 %copy-done.4 = bf16[4,256,256]{2,1,0:T(8,128)(2,1)S(1)} copy-done((bf16[4,256,256]{2,1,0:T(8,128)(2,1)S(1)}, bf16[4,256,256]{2,1,0:T(8,128)(2,1)}, u32[]{:S(2)}) %copy-start.4) | copy-done | bytes 524312
  7.4 0.0 copy-start.5
  7.4 1.2 %copy-done.5 = bf16[1,8,1,256,256]{4,3,2,1,0:T(8,128)(2,1)S(1)} copy-done((bf16[1,8,1,256,256]{4,3,2,1,0:T(8,128)(2,1)S(1)}, bf16[1,8,1,256,256]{4,3,2,1,0:T(8,128)(2,1)}, u32[]{:S(2)}) %copy-start.5) | copy-done | bytes 1048600
  8.6 0.0 copy-start.6
  8.6 0.9 %copy-done.6 = bf16[2,256,256]{2,1,0:T(8,128)(2,1)S(1)} copy-done((bf16[2,256,256]{2,1,0:T(8,128)(2,1)S(1)}, bf16[2,256,256]{2,1,0:T(8,128)(2,1)}, u32[]{:S(2)}) %copy-start.6) | copy-done | bytes 262168
  9.5 0.0 copy-start.9
  9.5 0.9 %copy-done.9 = bf16[256,256]{1,0:T(8,128)(2,1)S(1)} copy-done((bf16[256,256]{1,0:T(8,128)(2,1)S(1)}, bf16[256,256]{1,0:T(8,128)(2,1)}, u32[]{:S(2)}) %copy-start.9) | copy-done | bytes 131096
  10.5 0.0 copy-start.3
  10.5 0.0 copy-start.7
  10.5 0.0 copy-start.8
  10.5 1.4 %shard_map.104.after_ref.meas_ref = bf16[8,256,256]{2,1,0:T(8,128)(2,1)S(1)} custom-call(s32[18]{0:T(128)S(1)} %pad_add_fusion.info_ref, bf16[8,256,256]{2,1,0:T(8,128)(2,1)S(1)} %bitcast.13, bf16[256,256]{1,0:T(8,128)(2,1)S(1)} %copy-done.9, bf16[2,256,256]{2,1,0:T(8,128)(2,1)S(1)} %copy-done.6, bf16[4,320,256]{2,1,0:T(8,128)(2,1)S(1)} %copy-done.2, ...), custom_call_target="tpu_custom_call" | custom-call | flops 1048576 | bytes 4096 | tf_op jit(solution)/shard_map/pallas_call | solution.py:326
  11.8 1.8 %collective-permute-done.1.value_ref = bf16[2,256,512]{2,1,0:T(8,128)(2,1)S(1)} collective-permute-done((bf16[2,256,512]{2,1,0:T(8,128)(2,1)}, bf16[2,256,512]{2,1,0:T(8,128)(2,1)S(1)}, u32[]{:S(2)}, u32[]{:S(2)}) %collective-permute-start.1) | collective-permute-done | bytes 524320 | tf_op jit(solution)/shard_map/ppermute | solution.py:319
  13.7 1.5 %collective-permute-start.2 = (bf16[2,256,512]{2,1,0:T(8,128)(2,1)S(1)}, bf16[2,256,512]{2,1,0:T(8,128)(2,1)S(1)}, u32[]{:S(2)}, u32[]{:S(2)}) collective-permute-start(bf16[2,256,512]{2,1,0:T(8,128)(2,1)S(1)} %shard_map.105.halo_own_ref), channel_id=1, source_target_pairs={{0,1},{1,0},{2,3},{3,2},{4,5},{5,4},{6,7},{7,6},{8,9},{9,8},{10,11... | collective-permute-start | bytes 1572872 | tf_op jit(solution)/shard_map/ppermute | solution.py:314
  15.2 0.0 collective-permute-done.other_ref
  15.2 1.5 %collective-permute-done.2.halo_other_ref = bf16[2,256,512]{2,1,0:T(8,128)(2,1)S(1)} collective-permute-done((bf16[2,256,512]{2,1,0:T(8,128)(2,1)S(1)}, bf16[2,256,512]{2,1,0:T(8,128)(2,1)S(1)}, u32[]{:S(2)}, u32[]{:S(2)}) %collective-permute-start.2) | collective-permute-done | bytes 524320 | tf_op jit(solution)/shard_map/ppermute | solution.py:314
  16.7 0.0 copy-done.3
  16.7 0.0 copy-done.7
  16.8 0.0 copy-done.8
  16.8 5.6 %shard_map.106 = (bf16[2,8,2,256,256]{4,3,2,1,0:T(8,128)(2,1)S(1)}, f32[256,256]{1,0:T(8,128)S(1)}, bf16[256,256]{1,0:T(8,128)(2,1)S(1)}) custom-call(s32[18]{0:T(128)S(1)} %pad_add_fusion.info_ref, bf16[2,256,512]{2,1,0:T(8,128)(2,1)S(1)} %bitcast.16, bf16[2,256,512]{2,1,0:T(8,128)(2,1)S(1)} %collective-permute-done.other_ref, ...), custom_call_target="tpu_custom_call" | custom-call | flops 1048576 | bytes 4096 | tf_op jit(solution)/shard_map/pallas_call | solution.py:326
  22.4 0.0 copy-start
  22.4 0.4 collective-permute-start.3
  22.8 1.6 %shard_map.108 = (bf16[2,256,512]{2,1,0:T(8,128)(2,1)S(1)}, bf16[2,256,512]{2,1,0:T(8,128)(2,1)S(1)}, bf16[256,256]{1,0:T(8,128)(2,1)}) custom-call(s32[18]{0:T(128)S(1)} %pad_add_fusion.info_ref, bf16[2,8,2,256,256]{4,3,2,1,0:T(8,128)(2,1)S(1)} %get-tuple-element.10.grads_ref.after_ref, bf16[2,8,2,256,256]{4,3,2,1,0:T(8,128)(2,1)S(1)} %get-tuple-element.10.grads_ref.after_ref), custom_call_target="tpu_custom_call" | custom-call | flops 1048576 | bytes 4096 | tf_op jit(solution)/shard_map/pallas_call | solution.py:326
  24.4 0.0 copy-done
  24.4 0.4 collective-permute-start.5
  24.8 0.0 collective-permute-done.3
  24.8 7.8 %collective-permute-start.7 = (bf16[256,256]{1,0:T(8,128)(2,1)S(1)}, bf16[256,256]{1,0:T(8,128)(2,1)S(1)}, u32[]{:S(2)}, u32[]{:S(2)}) collective-permute-start(bf16[256,256]{1,0:T(8,128)(2,1)S(1)} %add_convert_fusion.3.after_ref), channel_id=1, source_target_pairs={{0,2},{2,0},{4,6},{6,4},{8,10},{10,8},{12,14},{14,12},{1,3},{3,1},... | collective-permute-start | bytes 393224 | tf_op jit(solution)/shard_map/ppermute | solution.py:392
  32.7 0.6 %collective-permute-start.4 = (bf16[2,256,512]{2,1,0:T(8,128)(2,1)S(1)}, bf16[2,256,512]{2,1,0:T(8,128)(2,1)S(1)}, u32[]{:S(2)}, u32[]{:S(2)}) collective-permute-start(bf16[2,256,512]{2,1,0:T(8,128)(2,1)S(1)} %get-tuple-element.14), channel_id=1, source_target_pairs={{0,1},{1,0},{2,3},{3,2},{4,5},{5,4},{6,7},{7,6},{8,9},{9,8},{10,11... | collective-permute-start | bytes 1572872 | tf_op jit(solution)/shard_map/ppermute | solution.py:314
  33.3 0.0 copy-start.1
  33.3 2.2 %copy-done.1 = bf16[2,8,2,256,256]{4,3,2,1,0:T(8,128)(2,1)S(1)} copy-done((bf16[2,8,2,256,256]{4,3,2,1,0:T(8,128)(2,1)S(1)}, bf16[2,8,2,256,256]{4,3,2,1,0:T(8,128)(2,1)}, u32[]{:S(2)}) %copy-start.1) | copy-done | bytes 4194328
  35.5 1.1 %shard_map.107 = (f32[2,256,512]{2,1,0:T(8,128)S(1)}, bf16[2,256,512]{2,1,0:T(8,128)(2,1)S(1)}, bf16[256,256]{1,0:T(8,128)(2,1)S(1)}) custom-call(s32[18]{0:T(128)S(1)} %pad_add_fusion.info_ref, bf16[2,8,2,256,256]{4,3,2,1,0:T(8,128)(2,1)S(1)} %copy-done.1, bf16[256,256]{1,0:T(8,128)(2,1)S(1)} %add_convert_fusion.3.after_ref), custom_call_target="tpu_custom_call" | custom-call | flops 1048576 | bytes 4096 | tf_op jit(solution)/shard_map/pallas_call | solution.py:326
  36.6 0.0 collective-permute-done.7
  36.6 0.1 add_convert_fusion.2
  36.6 0.1 collective-permute-start.8
  36.7 0.0 collective-permute-done.5
  36.7 0.1 add_convert_fusion
  36.9 1.3 %collective-permute-start.6 = (bf16[2,256,512]{2,1,0:T(8,128)(2,1)S(1)}, bf16[2,256,512]{2,1,0:T(8,128)(2,1)S(1)}, u32[]{:S(2)}, u32[]{:S(2)}) collective-permute-start(bf16[2,256,512]{2,1,0:T(8,128)(2,1)S(1)} %add_convert_fusion), channel_id=1, source_target_pairs={{0,2},{2,4},{4,6},{6,8},{8,10},{10,12},{12,14},{1,3},{3,5},{5,7},{... | collective-permute-start | bytes 1572872 | tf_op jit(solution)/shard_map/ppermute | solution.py:319
  38.2 3.0 %collective-permute-done.8 = bf16[256,256]{1,0:T(8,128)(2,1)S(1)} collective-permute-done((bf16[256,256]{1,0:T(8,128)(2,1)S(1)}, bf16[256,256]{1,0:T(8,128)(2,1)S(1)}, u32[]{:S(2)}, u32[]{:S(2)}) %collective-permute-start.8) | collective-permute-done | bytes 131104 | tf_op jit(solution)/shard_map/ppermute | solution.py:392
  41.2 0.8 %collective-permute-start.9 = (bf16[256,256]{1,0:T(8,128)(2,1)S(1)}, bf16[256,256]{1,0:T(8,128)(2,1)S(1)}, u32[]{:S(2)}, u32[]{:S(2)}) collective-permute-start(bf16[256,256]{1,0:T(8,128)(2,1)S(1)} %add_convert_fusion.1), channel_id=1, source_target_pairs={{0,8},{2,10},{4,12},{6,14},{8,0},{10,2},{12,4},{14,6},{1,9},{3,11}... | collective-permute-start | bytes 393224 | tf_op jit(solution)/shard_map/ppermute | solution.py:392
  42.1 0.0 collective-permute-done.4
  42.1 0.2 convert_add_fusion
  42.2 15.5 %collective-permute-done.9.value_ref = bf16[256,256]{1,0:T(8,128)(2,1)S(1)} collective-permute-done((bf16[256,256]{1,0:T(8,128)(2,1)S(1)}, bf16[256,256]{1,0:T(8,128)(2,1)S(1)}, u32[]{:S(2)}, u32[]{:S(2)}) %collective-permute-start.9) | collective-permute-done | bytes 131104 | tf_op jit(solution)/shard_map/ppermute | solution.py:392
  57.7 0.0 collective-permute-done.6.after_ref
  57.8 2.7 %collective-permute-start.10 = (f32[256,256]{1,0:T(8,128)S(1)}, f32[256,256]{1,0:T(8,128)S(1)}, u32[]{:S(2)}, u32[]{:S(2)}) collective-permute-start(f32[256,256]{1,0:T(8,128)S(1)} %get-tuple-element.19), channel_id=1, source_target_pairs={{0,1},{1,0},{2,3},{3,2},{4,5},{5,4},{6,7},{7,6},{8,9},{9,8},{10,11... | collective-permute-start | bytes 786440 | tf_op jit(solution)/shard_map/ppermute | solution.py:314
  60.5 1.1 %add_bitcast_fusion = f32[1,2,256,512]{3,2,1,0:T(8,128)} fusion(f32[2,256,512]{2,1,0:T(8,128)S(1)} %convert_add_fusion, bf16[2,256,512]{2,1,0:T(8,128)(2,1)S(1)} %collective-permute-done.6.after_ref), kind=kLoop, calls=%fused_computation | loop fusion | flops 524288 | bytes 2621440 | tf_op jit(solution)/shard_map/broadcast_in_dim | solution.py:407
  61.7 0.0 collective-permute-done.10
  61.7 0.8 %maximum_select_fusion = f32[2,256,256]{2,1,0:T(8,128)} fusion(f32[1,256,256]{2,1,0:T(8,128)S(1)} %bitcast.17, f32[1,256,256]{2,1,0:T(8,128)S(1)} %get-tuple-element.18, pred[]{:T(512)S(6)} %eq.3), kind=kLoop, calls=%fused_computation.3 | loop fusion | flops 393216 | bytes 1048577 | tf_op jit(solution)/shard_map/jit(_where)/select_n | solution.py:406
  (5 shorter events, 0.1 us)
Async XLA Ops:
  0.6 13.0 %collective-permute-start.1 = (bf16[2,256,512]{2,1,0:T(8,128)(2,1)}, bf16[2,256,512]{2,1,0:T(8,128)(2,1)S(1)}, u32[]{:S(2)}, u32[]{:S(2)}) collective-permute-start(bf16[2,256,512]{2,1,0:T(8,128)(2,1)} %bitcast.14), channel_id=1, source_target_pairs={{2,0},{4,2},{6,4},{8,6},{10,8},{12,10},{14,12},{3,1},{5,3},{7,5},{... | collective-permute-start | bytes 1572872 | tf_op jit(solution)/shard_map/ppermute | solution.py:319
  2.8 12.4 %collective-permute-start = (bf16[2,256,512]{2,1,0:T(8,128)(2,1)}, bf16[2,256,512]{2,1,0:T(8,128)(2,1)S(1)}, u32[]{:S(2)}, u32[]{:S(2)}) collective-permute-start(bf16[2,256,512]{2,1,0:T(8,128)(2,1)} %bitcast.15), channel_id=1, source_target_pairs={{0,1},{1,0},{2,3},{3,2},{4,5},{5,4},{6,7},{7,6},{8,9},{9,8},{10,11... | collective-permute-start | bytes 1572872 | tf_op jit(solution)/shard_map/ppermute | solution.py:314
  5.2 1.1 %copy-start.2 = (bf16[4,320,256]{2,1,0:T(8,128)(2,1)S(1)}, bf16[4,320,256]{2,1,0:T(8,128)(2,1)}, u32[]{:S(2)}) copy-start(bf16[4,320,256]{2,1,0:T(8,128)(2,1)} %constant.35.clone.prop_ref) | copy-start | bytes 1966084
  6.3 1.0 %copy-start.4 = (bf16[4,256,256]{2,1,0:T(8,128)(2,1)S(1)}, bf16[4,256,256]{2,1,0:T(8,128)(2,1)}, u32[]{:S(2)}) copy-start(bf16[4,256,256]{2,1,0:T(8,128)(2,1)} %constant.36.clone.four_ref) | copy-start | bytes 1572868
  7.4 1.2 %copy-start.5 = (bf16[1,8,1,256,256]{4,3,2,1,0:T(8,128)(2,1)S(1)}, bf16[1,8,1,256,256]{4,3,2,1,0:T(8,128)(2,1)}, u32[]{:S(2)}) copy-start(bf16[1,8,1,256,256]{4,3,2,1,0:T(8,128)(2,1)} %param.11) | copy-start | bytes 3145732
  8.6 0.9 %copy-start.6 = (bf16[2,256,256]{2,1,0:T(8,128)(2,1)S(1)}, bf16[2,256,256]{2,1,0:T(8,128)(2,1)}, u32[]{:S(2)}) copy-start(bf16[2,256,256]{2,1,0:T(8,128)(2,1)} %probe_ref.3) | copy-start | bytes 786436
  9.5 0.9 %copy-start.9 = (bf16[256,256]{1,0:T(8,128)(2,1)S(1)}, bf16[256,256]{1,0:T(8,128)(2,1)}, u32[]{:S(2)}) copy-start(bf16[256,256]{1,0:T(8,128)(2,1)} %constant.37.clone.perm_ref) | copy-start | bytes 393220
  10.5 6.3 %copy-start.3 = (bf16[4,320,256]{2,1,0:T(8,128)(2,1)S(1)}, bf16[4,320,256]{2,1,0:T(8,128)(2,1)}, u32[]{:S(2)}) copy-start(bf16[4,320,256]{2,1,0:T(8,128)(2,1)} %constant.35.clone.prop_ref) | copy-start | bytes 1966084
  10.5 6.3 %copy-start.7 = (bf16[2,256,256]{2,1,0:T(8,128)(2,1)S(1)}, bf16[2,256,256]{2,1,0:T(8,128)(2,1)}, u32[]{:S(2)}) copy-start(bf16[2,256,256]{2,1,0:T(8,128)(2,1)} %probe_ref.3) | copy-start | bytes 786436
  10.5 6.3 %copy-start.8 = (bf16[1,2,256,512]{3,2,1,0:T(8,128)(2,1)S(1)}, bf16[1,2,256,512]{3,2,1,0:T(8,128)(2,1)}, u32[]{:S(2)}) copy-start(bf16[1,2,256,512]{3,2,1,0:T(8,128)(2,1)} %param.9) | copy-start | bytes 1572868
  13.7 3.1 %collective-permute-start.2 = (bf16[2,256,512]{2,1,0:T(8,128)(2,1)S(1)}, bf16[2,256,512]{2,1,0:T(8,128)(2,1)S(1)}, u32[]{:S(2)}, u32[]{:S(2)}) collective-permute-start(bf16[2,256,512]{2,1,0:T(8,128)(2,1)S(1)} %shard_map.105.halo_own_ref), channel_id=1, source_target_pairs={{0,1},{1,0},{2,3},{3,2},{4,5},{5,4},{6,7},{7,6},{8,9},{9,8},{10,11... | collective-permute-start | bytes 1572872 | tf_op jit(solution)/shard_map/ppermute | solution.py:314
  22.4 2.0 %copy-start = (bf16[2,8,2,256,256]{4,3,2,1,0:T(8,128)(2,1)}, bf16[2,8,2,256,256]{4,3,2,1,0:T(8,128)(2,1)S(1)}, u32[]{:S(2)}) copy-start(bf16[2,8,2,256,256]{4,3,2,1,0:T(8,128)(2,1)S(1)} %get-tuple-element.10.grads_ref.after_ref) | copy-start | bytes 12582916
  22.4 2.4 %collective-permute-start.3 = (bf16[256,256]{1,0:T(8,128)(2,1)S(1)}, bf16[256,256]{1,0:T(8,128)(2,1)S(1)}, u32[]{:S(2)}, u32[]{:S(2)}) collective-permute-start(bf16[256,256]{1,0:T(8,128)(2,1)S(1)} %get-tuple-element.12), channel_id=1, source_target_pairs={{0,1},{1,0},{2,3},{3,2},{4,5},{5,4},{6,7},{7,6},{8,9},{9,8},{10,11... | collective-permute-start | bytes 393224 | tf_op jit(solution)/shard_map/ppermute | solution.py:314
  24.4 12.3 %collective-permute-start.5 = (bf16[2,256,512]{2,1,0:T(8,128)(2,1)S(1)}, bf16[2,256,512]{2,1,0:T(8,128)(2,1)S(1)}, u32[]{:S(2)}, u32[]{:S(2)}) collective-permute-start(bf16[2,256,512]{2,1,0:T(8,128)(2,1)S(1)} %get-tuple-element.16), channel_id=1, source_target_pairs={{0,1},{1,0},{2,3},{3,2},{4,5},{5,4},{6,7},{7,6},{8,9},{9,8},{10,11... | collective-permute-start | bytes 1572872 | tf_op jit(solution)/shard_map/ppermute | solution.py:314
  24.8 11.7 %collective-permute-start.7 = (bf16[256,256]{1,0:T(8,128)(2,1)S(1)}, bf16[256,256]{1,0:T(8,128)(2,1)S(1)}, u32[]{:S(2)}, u32[]{:S(2)}) collective-permute-start(bf16[256,256]{1,0:T(8,128)(2,1)S(1)} %add_convert_fusion.3.after_ref), channel_id=1, source_target_pairs={{0,2},{2,0},{4,6},{6,4},{8,10},{10,8},{12,14},{14,12},{1,3},{3,1},... | collective-permute-start | bytes 393224 | tf_op jit(solution)/shard_map/ppermute | solution.py:392
  32.7 9.4 %collective-permute-start.4 = (bf16[2,256,512]{2,1,0:T(8,128)(2,1)S(1)}, bf16[2,256,512]{2,1,0:T(8,128)(2,1)S(1)}, u32[]{:S(2)}, u32[]{:S(2)}) collective-permute-start(bf16[2,256,512]{2,1,0:T(8,128)(2,1)S(1)} %get-tuple-element.14), channel_id=1, source_target_pairs={{0,1},{1,0},{2,3},{3,2},{4,5},{5,4},{6,7},{7,6},{8,9},{9,8},{10,11... | collective-permute-start | bytes 1572872 | tf_op jit(solution)/shard_map/ppermute | solution.py:314
  33.3 2.2 %copy-start.1 = (bf16[2,8,2,256,256]{4,3,2,1,0:T(8,128)(2,1)S(1)}, bf16[2,8,2,256,256]{4,3,2,1,0:T(8,128)(2,1)}, u32[]{:S(2)}) copy-start(bf16[2,8,2,256,256]{4,3,2,1,0:T(8,128)(2,1)} %copy-done) | copy-start | bytes 12582916
  36.6 4.6 %collective-permute-start.8 = (bf16[256,256]{1,0:T(8,128)(2,1)S(1)}, bf16[256,256]{1,0:T(8,128)(2,1)S(1)}, u32[]{:S(2)}, u32[]{:S(2)}) collective-permute-start(bf16[256,256]{1,0:T(8,128)(2,1)S(1)} %add_convert_fusion.2), channel_id=1, source_target_pairs={{0,4},{2,6},{4,0},{6,2},{8,12},{10,14},{12,8},{14,10},{1,5},{3,7},... | collective-permute-start | bytes 393224 | tf_op jit(solution)/shard_map/ppermute | solution.py:392
  36.9 20.9 %collective-permute-start.6 = (bf16[2,256,512]{2,1,0:T(8,128)(2,1)S(1)}, bf16[2,256,512]{2,1,0:T(8,128)(2,1)S(1)}, u32[]{:S(2)}, u32[]{:S(2)}) collective-permute-start(bf16[2,256,512]{2,1,0:T(8,128)(2,1)S(1)} %add_convert_fusion), channel_id=1, source_target_pairs={{0,2},{2,4},{4,6},{6,8},{8,10},{10,12},{12,14},{1,3},{3,5},{5,7},{... | collective-permute-start | bytes 1572872 | tf_op jit(solution)/shard_map/ppermute | solution.py:319
  41.2 16.5 %collective-permute-start.9 = (bf16[256,256]{1,0:T(8,128)(2,1)S(1)}, bf16[256,256]{1,0:T(8,128)(2,1)S(1)}, u32[]{:S(2)}, u32[]{:S(2)}) collective-permute-start(bf16[256,256]{1,0:T(8,128)(2,1)S(1)} %add_convert_fusion.1), channel_id=1, source_target_pairs={{0,8},{2,10},{4,12},{6,14},{8,0},{10,2},{12,4},{14,6},{1,9},{3,11}... | collective-permute-start | bytes 393224 | tf_op jit(solution)/shard_map/ppermute | solution.py:392
  57.8 3.9 %collective-permute-start.10 = (f32[256,256]{1,0:T(8,128)S(1)}, f32[256,256]{1,0:T(8,128)S(1)}, u32[]{:S(2)}, u32[]{:S(2)}) collective-permute-start(f32[256,256]{1,0:T(8,128)S(1)} %get-tuple-element.19), channel_id=1, source_target_pairs={{0,1},{1,0},{2,3},{3,2},{4,5},{5,4},{6,7},{7,6},{8,9},{9,8},{10,11... | collective-permute-start | bytes 786440 | tf_op jit(solution)/shard_map/ppermute | solution.py:314

commit v4 on v3

--- a/solution.py
+++ b/solution.py
@@ -211,20 +211,19 @@
 
     def visit(step, _):
         group = list(members(step, live))
-        for g, (slot, _) in enumerate(group):
-            place = place_of(info_ref, slots, slot)
+        places = [place_of(info_ref, slots, slot) for slot, _ in group]
+        for g, place in enumerate(places):
             window(ext_a, win_a.at[g], place)
-            window(ext_b, win_b.at[g], place)
             for j in range(steps):
                 span = slice(j * CHUNK, (j + 1) * CHUNK)
                 pr, pi = pro[0, span], pro[1, span]
                 wr, wi = win_a[g, 0, span], win_a[g, 1, span]
                 put(x_a.at[g], j * CHUNK, pr * wr - pi * wi, pr * wi + pi * wr)
-        for g in range(GROUP):
             at = banded(prop_ref, 0, x_a[g])
             for j in range(steps):
                 put(x_b.at[g], j * CHUNK, *at(j))
         for g in range(GROUP):
+            window(ext_b, win_b.at[g], places[g])
             at = banded(prop_ref, 0, x_b[g])
             for j in range(steps):
                 span = slice(j * CHUNK, (j + 1) * CHUNK)
@@ -320,6 +319,7 @@
 
 
 def call(mib, body, results, operands, info, scratch, loose=(), alias=None):
+    moved = 2**22 if mib == 13 else 2**12
     vmem = pl.BlockSpec(memory_space=pltpu.VMEM)
     smem = pl.BlockSpec(memory_space=pltpu.SMEM)
     spots = [smem] * len(info) + [pl.BlockSpec(memory_space=pl.ANY) if i in loose else vmem for i in range(len(operands))]
@@ -330,7 +330,7 @@
         out_specs=(pl.BlockSpec(memory_space=pl.ANY) if alias else vmem,) * len(results),
         scratch_shapes=scratch,
         input_output_aliases=alias or {},
-        cost_estimate=pl.CostEstimate(flops=2**20, bytes_accessed=2**12, transcendentals=0),
+        cost_estimate=pl.CostEstimate(flops=2**20, bytes_accessed=moved, transcendentals=0),
         compiler_params=pltpu.CompilerParams(vmem_limit_bytes=mib * MIB),
     )(*info, *operands)
 
@@ -375,29 +375,27 @@
     rows = (2, strip, ny)
     flat = sds((size, size), bf16)
     away_strip, away_tail, token = call(
-        12,
+        13,
         functools.partial(placing_kernel, False),
         (sds(rows, bf16), sds(rows, bf16), flat), (grads, grads), info, [ext], loose=(1,),
     )
     part = mine + swap(theirs).astype(f32)
     part = part.astype(bf16)
     own_strip, own_tail, token = call(
-        12,
+        13,
         functools.partial(placing_kernel, True),
         (sds(rows, f32), sds(rows, bf16), flat), (grads, part), info, [ext], loose=(1,),
     )
-    above = shift_tile((own_tail.astype(f32) + swap(away_tail).astype(f32)).astype(bf16), 1)
     step = 1
     while step < peers:
         got = lax.ppermute(part, "tile", [(i, i ^ step) for i in range(peers)])
-        if 2 * step >= peers:
-            (got,) = call(4, pass_kernel, (sds(got.shape, bf16),), (above, got), (), [], loose=(0, 1), alias={1: 0})
         total = part.astype(f32) + got.astype(f32)
         if step == 1:
             total = total + token.astype(f32)
         part = total.astype(bf16)
         step *= 2
 
+    above = shift_tile((own_tail.astype(f32) + swap(away_tail).astype(f32)).astype(bf16), 1)
     owned = lax.optimization_barrier(own_strip + swap(away_strip).astype(f32))
     owned = owned + above.astype(f32)
 

time: 62.3 us -> 61.2 us (0.982)
  the two profiles are of different devices: /device:TPU:29 before, /device:TPU:16 now
where the time goes in v4:
time: 61.2 us; the launch traced here: 60.3 us
  waiting for transfers between devices  27.5 us (45%)
  Pallas kernels  16.4 us (27%)
  starting transfers between devices  6.56 us (11%)
  local copies, waits for them, and re-layouts  5.22 us (9%)
  other arithmetic  3.2 us (5%)
  between operations  1.43 us (2%)
    pallas_call x5, Pallas kernels, call(): pl.pallas_call(body, out_shape=tuple(results), in_specs=spots, out_specs=...  16.4 us
    ppermute x2, waiting for transfers between devices, shift_tile(): lax.ppermute(value, 'tile', [(i, i + by) for i in range(peers) if 0 <= i...  14 us
    ppermute x3, waiting for transfers between devices, local(): got = lax.ppermute(part, 'tile', [(i, i ^ step) for i in range(peers)])  9.07 us
    ppermute x2, starting transfers between devices, shift_tile(): lax.ppermute(value, 'tile', [(i, i + by) for i in range(peers) if 0 <= i...  5.58 us
    unnamed x16, local copies, waits for them, and re-layouts  5.22 us
    ppermute x6, waiting for transfers between devices, swap(): return lax.ppermute(value, 'pos', [(0, 1), (1, 0)])  4.41 us
  transfers between devices with their start and end apart: 11, of which 8 were waited for; matrix products, arithmetic and copies ran while one was open for 3% of the time, Pallas kernels for 10%

profile of v4, /device:TPU:16, one launch (start us, length us, event | category | flops | bytes accessed | tf_op | source)
XLA Modules:
  0.0 60.3 jit_solution(17461844819657537106)
XLA Ops:
  0.6 3.3 %collective-permute-start.1 = (bf16[2,256,512]{2,1,0:T(8,128)(2,1)}, bf16[2,256,512]{2,1,0:T(8,128)(2,1)S(1)}, u32[]{:S(2)}, u32[]{:S(2)}) collective-permute-start(bf16[2,256,512]{2,1,0:T(8,128)(2,1)} %bitcast.14), channel_id=1, source_target_pairs={{2,0},{4,2},{6,4},{8,6},{10,8},{12,10},{14,12},{3,1},{5,3},{7,5},{... | collective-permute-start | bytes 1572872 | tf_op jit(solution)/shard_map/ppermute | solution.py:318
  4.0 0.1 collective-permute-start
  4.7 0.8 %pad_add_fusion.info_ref = s32[18]{0:T(128)S(1)} fusion(s32[8]{0:T(128)} %bitcast.18, s32[8]{0:T(128)} %bitcast.19, s32[1]{0:T(128)} %bitcast.2, s32[1]{0:T(128)} %bitcast), kind=kLoop, calls=%fused_computation.8 | loop fusion | flops 54 | bytes 144 | tf_op jit(solution)/shard_map/concatenate | solution.py:349
  5.4 0.0 copy-start
  5.4 1.1 %copy-done = bf16[4,320,256]{2,1,0:T(8,128)(2,1)S(1)} copy-done((bf16[4,320,256]{2,1,0:T(8,128)(2,1)S(1)}, bf16[4,320,256]{2,1,0:T(8,128)(2,1)}, u32[]{:S(2)}) %copy-start) | copy-done | bytes 655384
  6.5 0.0 copy-start.2
  6.5 1.0 %copy-done.2 = bf16[4,256,256]{2,1,0:T(8,128)(2,1)S(1)} copy-done((bf16[4,256,256]{2,1,0:T(8,128)(2,1)S(1)}, bf16[4,256,256]{2,1,0:T(8,128)(2,1)}, u32[]{:S(2)}) %copy-start.2) | copy-done | bytes 524312
  7.6 0.0 copy-start.3
  7.6 1.2 %copy-done.3 = bf16[1,8,1,256,256]{4,3,2,1,0:T(8,128)(2,1)S(1)} copy-done((bf16[1,8,1,256,256]{4,3,2,1,0:T(8,128)(2,1)S(1)}, bf16[1,8,1,256,256]{4,3,2,1,0:T(8,128)(2,1)}, u32[]{:S(2)}) %copy-start.3) | copy-done | bytes 1048600
  8.8 0.0 copy-start.4
  8.8 0.9 %copy-done.4 = bf16[2,256,256]{2,1,0:T(8,128)(2,1)S(1)} copy-done((bf16[2,256,256]{2,1,0:T(8,128)(2,1)S(1)}, bf16[2,256,256]{2,1,0:T(8,128)(2,1)}, u32[]{:S(2)}) %copy-start.4) | copy-done | bytes 262168
  9.8 0.0 copy-start.7
  9.8 0.9 %copy-done.7 = bf16[256,256]{1,0:T(8,128)(2,1)S(1)} copy-done((bf16[256,256]{1,0:T(8,128)(2,1)S(1)}, bf16[256,256]{1,0:T(8,128)(2,1)}, u32[]{:S(2)}) %copy-start.7) | copy-done | bytes 131096
  10.7 0.0 copy-start.1
  10.7 0.0 copy-start.5
  10.7 0.0 copy-start.6
  10.7 1.4 %shard_map.104.after_ref.meas_ref = bf16[8,256,256]{2,1,0:T(8,128)(2,1)S(1)} custom-call(s32[18]{0:T(128)S(1)} %pad_add_fusion.info_ref, bf16[8,256,256]{2,1,0:T(8,128)(2,1)S(1)} %bitcast.13, bf16[256,256]{1,0:T(8,128)(2,1)S(1)} %copy-done.7, bf16[2,256,256]{2,1,0:T(8,128)(2,1)S(1)} %copy-done.4, bf16[4,320,256]{2,1,0:T(8,128)(2,1)S(1)} %copy-done, ...), custom_call_target="tpu_custom_call" | custom-call | flops 1048576 | bytes 4096 | tf_op jit(solution)/shard_map/pallas_call | solution.py:326
  12.0 4.4 %collective-permute-done.1.value_ref = bf16[2,256,512]{2,1,0:T(8,128)(2,1)S(1)} collective-permute-done((bf16[2,256,512]{2,1,0:T(8,128)(2,1)}, bf16[2,256,512]{2,1,0:T(8,128)(2,1)S(1)}, u32[]{:S(2)}, u32[]{:S(2)}) %collective-permute-start.1) | collective-permute-done | bytes 524320 | tf_op jit(solution)/shard_map/ppermute | solution.py:318
  16.4 0.0 collective-permute-start.2
  16.4 0.0 collective-permute-done.other_ref
  16.4 1.9 %collective-permute-done.2.halo_other_ref = bf16[2,256,512]{2,1,0:T(8,128)(2,1)S(1)} collective-permute-done((bf16[2,256,512]{2,1,0:T(8,128)(2,1)S(1)}, bf16[2,256,512]{2,1,0:T(8,128)(2,1)S(1)}, u32[]{:S(2)}, u32[]{:S(2)}) %collective-permute-start.2) | collective-permute-done | bytes 524320 | tf_op jit(solution)/shard_map/ppermute | solution.py:313
  18.3 0.0 copy-done.1
  18.3 0.0 copy-done.5
  18.3 0.0 copy-done.6
  18.3 10.5 %shard_map.106 = (bf16[2,8,2,256,256]{4,3,2,1,0:T(8,128)(2,1)S(1)}, f32[256,256]{1,0:T(8,128)S(1)}, bf16[256,256]{1,0:T(8,128)(2,1)S(1)}) custom-call(s32[18]{0:T(128)S(1)} %pad_add_fusion.info_ref, bf16[2,256,512]{2,1,0:T(8,128)(2,1)S(1)} %bitcast.16, bf16[2,256,512]{2,1,0:T(8,128)(2,1)S(1)} %collective-permute-done.other_ref, ...), custom_call_target="tpu_custom_call" | custom-call | flops 1048576 | bytes 4096 | tf_op jit(solution)/shard_map/pallas_call | solution.py:326
  28.8 0.2 collective-permute-start.3
  29.0 1.2 %collective-permute-done.3 = bf16[256,256]{1,0:T(8,128)(2,1)S(1)} collective-permute-done((bf16[256,256]{1,0:T(8,128)(2,1)S(1)}, bf16[256,256]{1,0:T(8,128)(2,1)S(1)}, u32[]{:S(2)}, u32[]{:S(2)}) %collective-permute-start.3) | collective-permute-done | bytes 131104 | tf_op jit(solution)/shard_map/ppermute | solution.py:313
  30.3 0.1 collective-permute-start.7
  30.3 2.5 %shard_map.108 = (bf16[2,256,512]{2,1,0:T(8,128)(2,1)S(1)}, bf16[2,256,512]{2,1,0:T(8,128)(2,1)S(1)}, bf16[256,256]{1,0:T(8,128)(2,1)}) custom-call(s32[18]{0:T(128)S(1)} %pad_add_fusion.info_ref, bf16[2,8,2,256,256]{4,3,2,1,0:T(8,128)(2,1)S(1)} %get-tuple-element.10.grads_ref.after_ref, bf16[2,8,2,256,256]{4,3,2,1,0:T(8,128)(2,1)S(1)} %get-tuple-element.10.grads_ref.after_ref), custom_call_target="tpu_custom_call" | custom-call | flops 1048576 | bytes 4194304 | tf_op jit(solution)/shard_map/pallas_call | solution.py:326
  32.9 0.2 collective-permute-start.5
  33.1 2.1 %shard_map.107 = (f32[2,256,512]{2,1,0:T(8,128)S(1)}, bf16[2,256,512]{2,1,0:T(8,128)(2,1)S(1)}, bf16[256,256]{1,0:T(8,128)(2,1)S(1)}) custom-call(s32[18]{0:T(128)S(1)} %pad_add_fusion.info_ref, bf16[2,8,2,256,256]{4,3,2,1,0:T(8,128)(2,1)S(1)} %get-tuple-element.10.grads_ref.after_ref, bf16[256,256]{1,0:T(8,128)(2,1)S(1)} %add_convert_fusion.3.after_ref), custom_call_target="tpu_custom_call" | custom-call | flops 1048576 | bytes 4194304 | tf_op jit(solution)/shard_map/pallas_call | solution.py:326
  35.1 0.8 %collective-permute-done.7 = bf16[256,256]{1,0:T(8,128)(2,1)S(1)} collective-permute-done((bf16[256,256]{1,0:T(8,128)(2,1)S(1)}, bf16[256,256]{1,0:T(8,128)(2,1)S(1)}, u32[]{:S(2)}, u32[]{:S(2)}) %collective-permute-start.7) | collective-permute-done | bytes 131104 | tf_op jit(solution)/shard_map/ppermute | solution.py:391
  35.9 0.1 add_convert_fusion.2
  36.0 0.1 collective-permute-start.8
  36.0 0.1 collective-permute-start.4
  36.1 4.9 %collective-permute-done.8 = bf16[256,256]{1,0:T(8,128)(2,1)S(1)} collective-permute-done((bf16[256,256]{1,0:T(8,128)(2,1)S(1)}, bf16[256,256]{1,0:T(8,128)(2,1)S(1)}, u32[]{:S(2)}, u32[]{:S(2)}) %collective-permute-start.8) | collective-permute-done | bytes 131104 | tf_op jit(solution)/shard_map/ppermute | solution.py:391
  41.0 0.2 collective-permute-start.9
  41.2 0.0 collective-permute-done.5
  41.2 0.1 add_convert_fusion
  41.4 2.3 %collective-permute-start.6 = (bf16[2,256,512]{2,1,0:T(8,128)(2,1)S(1)}, bf16[2,256,512]{2,1,0:T(8,128)(2,1)S(1)}, u32[]{:S(2)}, u32[]{:S(2)}) collective-permute-start(bf16[2,256,512]{2,1,0:T(8,128)(2,1)S(1)} %add_convert_fusion), channel_id=1, source_target_pairs={{0,2},{2,4},{4,6},{6,8},{8,10},{10,12},{12,14},{1,3},{3,5},{5,7},{... | collective-permute-start | bytes 1572872 | tf_op jit(solution)/shard_map/ppermute | solution.py:318
  43.6 3.4 %collective-permute-done.9 = bf16[256,256]{1,0:T(8,128)(2,1)S(1)} collective-permute-done((bf16[256,256]{1,0:T(8,128)(2,1)S(1)}, bf16[256,256]{1,0:T(8,128)(2,1)S(1)}, u32[]{:S(2)}, u32[]{:S(2)}) %collective-permute-start.9) | collective-permute-done | bytes 131104 | tf_op jit(solution)/shard_map/ppermute | solution.py:391
  47.1 0.1 collective-permute-start.10
  47.2 0.0 collective-permute-done.4
  47.2 0.2 convert_add_fusion
  47.4 1.3 %collective-permute-done.10 = f32[256,256]{1,0:T(8,128)S(1)} collective-permute-done((f32[256,256]{1,0:T(8,128)S(1)}, f32[256,256]{1,0:T(8,128)S(1)}, u32[]{:S(2)}, u32[]{:S(2)}) %collective-permute-start.10) | collective-permute-done | bytes 262176 | tf_op jit(solution)/shard_map/ppermute | solution.py:313
  48.7 0.8 %maximum_select_fusion = f32[2,256,256]{2,1,0:T(8,128)} fusion(f32[1,256,256]{2,1,0:T(8,128)S(1)} %bitcast.17, f32[1,256,256]{2,1,0:T(8,128)S(1)} %get-tuple-element.18, pred[]{:T(512)S(6)} %eq.3), kind=kLoop, calls=%fused_computation.3 | loop fusion | flops 393216 | bytes 1048577 | tf_op jit(solution)/shard_map/jit(_where)/select_n | solution.py:404
  49.5 9.6 %collective-permute-done.6 = bf16[2,256,512]{2,1,0:T(8,128)(2,1)S(1)} collective-permute-done((bf16[2,256,512]{2,1,0:T(8,128)(2,1)S(1)}, bf16[2,256,512]{2,1,0:T(8,128)(2,1)S(1)}, u32[]{:S(2)}, u32[]{:S(2)}) %collective-permute-start.6) | collective-permute-done | bytes 524320 | tf_op jit(solution)/shard_map/ppermute | solution.py:318
  59.2 1.2 %add_bitcast_fusion = f32[1,2,256,512]{3,2,1,0:T(8,128)} fusion(f32[2,256,512]{2,1,0:T(8,128)S(1)} %convert_add_fusion, bf16[2,256,512]{2,1,0:T(8,128)(2,1)S(1)} %collective-permute-done.6), kind=kLoop, calls=%fused_computation | loop fusion | flops 524288 | bytes 2621440 | tf_op jit(solution)/shard_map/broadcast_in_dim | solution.py:405
  (4 shorter events, 0.1 us)
Async XLA Ops:
  0.6 15.8 %collective-permute-start.1 = (bf16[2,256,512]{2,1,0:T(8,128)(2,1)}, bf16[2,256,512]{2,1,0:T(8,128)(2,1)S(1)}, u32[]{:S(2)}, u32[]{:S(2)}) collective-permute-start(bf16[2,256,512]{2,1,0:T(8,128)(2,1)} %bitcast.14), channel_id=1, source_target_pairs={{2,0},{4,2},{6,4},{8,6},{10,8},{12,10},{14,12},{3,1},{5,3},{7,5},{... | collective-permute-start | bytes 1572872 | tf_op jit(solution)/shard_map/ppermute | solution.py:318
  4.0 12.5 %collective-permute-start = (bf16[2,256,512]{2,1,0:T(8,128)(2,1)}, bf16[2,256,512]{2,1,0:T(8,128)(2,1)S(1)}, u32[]{:S(2)}, u32[]{:S(2)}) collective-permute-start(bf16[2,256,512]{2,1,0:T(8,128)(2,1)} %bitcast.15), channel_id=1, source_target_pairs={{0,1},{1,0},{2,3},{3,2},{4,5},{5,4},{6,7},{7,6},{8,9},{9,8},{10,11... | collective-permute-start | bytes 1572872 | tf_op jit(solution)/shard_map/ppermute | solution.py:313
  5.4 1.1 %copy-start = (bf16[4,320,256]{2,1,0:T(8,128)(2,1)S(1)}, bf16[4,320,256]{2,1,0:T(8,128)(2,1)}, u32[]{:S(2)}) copy-start(bf16[4,320,256]{2,1,0:T(8,128)(2,1)} %constant.35.clone.prop_ref) | copy-start | bytes 1966084
  6.5 1.0 %copy-start.2 = (bf16[4,256,256]{2,1,0:T(8,128)(2,1)S(1)}, bf16[4,256,256]{2,1,0:T(8,128)(2,1)}, u32[]{:S(2)}) copy-start(bf16[4,256,256]{2,1,0:T(8,128)(2,1)} %constant.36.clone.four_ref) | copy-start | bytes 1572868
  7.6 1.2 %copy-start.3 = (bf16[1,8,1,256,256]{4,3,2,1,0:T(8,128)(2,1)S(1)}, bf16[1,8,1,256,256]{4,3,2,1,0:T(8,128)(2,1)}, u32[]{:S(2)}) copy-start(bf16[1,8,1,256,256]{4,3,2,1,0:T(8,128)(2,1)} %param.11) | copy-start | bytes 3145732
  8.8 0.9 %copy-start.4 = (bf16[2,256,256]{2,1,0:T(8,128)(2,1)S(1)}, bf16[2,256,256]{2,1,0:T(8,128)(2,1)}, u32[]{:S(2)}) copy-start(bf16[2,256,256]{2,1,0:T(8,128)(2,1)} %probe_ref.3) | copy-start | bytes 786436
  9.8 0.9 %copy-start.7 = (bf16[256,256]{1,0:T(8,128)(2,1)S(1)}, bf16[256,256]{1,0:T(8,128)(2,1)}, u32[]{:S(2)}) copy-start(bf16[256,256]{1,0:T(8,128)(2,1)} %constant.37.clone.perm_ref) | copy-start | bytes 393220
  10.7 7.7 %copy-start.1 = (bf16[4,320,256]{2,1,0:T(8,128)(2,1)S(1)}, bf16[4,320,256]{2,1,0:T(8,128)(2,1)}, u32[]{:S(2)}) copy-start(bf16[4,320,256]{2,1,0:T(8,128)(2,1)} %constant.35.clone.prop_ref) | copy-start | bytes 1966084
  10.7 7.7 %copy-start.5 = (bf16[2,256,256]{2,1,0:T(8,128)(2,1)S(1)}, bf16[2,256,256]{2,1,0:T(8,128)(2,1)}, u32[]{:S(2)}) copy-start(bf16[2,256,256]{2,1,0:T(8,128)(2,1)} %probe_ref.3) | copy-start | bytes 786436
  10.7 7.7 %copy-start.6 = (bf16[1,2,256,512]{3,2,1,0:T(8,128)(2,1)S(1)}, bf16[1,2,256,512]{3,2,1,0:T(8,128)(2,1)}, u32[]{:S(2)}) copy-start(bf16[1,2,256,512]{3,2,1,0:T(8,128)(2,1)} %param.9) | copy-start | bytes 1572868
  16.4 1.9 %collective-permute-start.2 = (bf16[2,256,512]{2,1,0:T(8,128)(2,1)S(1)}, bf16[2,256,512]{2,1,0:T(8,128)(2,1)S(1)}, u32[]{:S(2)}, u32[]{:S(2)}) collective-permute-start(bf16[2,256,512]{2,1,0:T(8,128)(2,1)S(1)} %shard_map.105.halo_own_ref), channel_id=1, source_target_pairs={{0,1},{1,0},{2,3},{3,2},{4,5},{5,4},{6,7},{7,6},{8,9},{9,8},{10,11... | collective-permute-start | bytes 1572872 | tf_op jit(solution)/shard_map/ppermute | solution.py:313
  28.8 1.4 %collective-permute-start.3 = (bf16[256,256]{1,0:T(8,128)(2,1)S(1)}, bf16[256,256]{1,0:T(8,128)(2,1)S(1)}, u32[]{:S(2)}, u32[]{:S(2)}) collective-permute-start(bf16[256,256]{1,0:T(8,128)(2,1)S(1)} %get-tuple-element.12), channel_id=1, source_target_pairs={{0,1},{1,0},{2,3},{3,2},{4,5},{5,4},{6,7},{7,6},{8,9},{9,8},{10,11... | collective-permute-start | bytes 393224 | tf_op jit(solution)/shard_map/ppermute | solution.py:313
  30.3 5.6 %collective-permute-start.7 = (bf16[256,256]{1,0:T(8,128)(2,1)S(1)}, bf16[256,256]{1,0:T(8,128)(2,1)S(1)}, u32[]{:S(2)}, u32[]{:S(2)}) collective-permute-start(bf16[256,256]{1,0:T(8,128)(2,1)S(1)} %add_convert_fusion.3.after_ref), channel_id=1, source_target_pairs={{0,2},{2,0},{4,6},{6,4},{8,10},{10,8},{12,14},{14,12},{1,3},{3,1},... | collective-permute-start | bytes 393224 | tf_op jit(solution)/shard_map/ppermute | solution.py:391
  32.9 8.4 %collective-permute-start.5 = (bf16[2,256,512]{2,1,0:T(8,128)(2,1)S(1)}, bf16[2,256,512]{2,1,0:T(8,128)(2,1)S(1)}, u32[]{:S(2)}, u32[]{:S(2)}) collective-permute-start(bf16[2,256,512]{2,1,0:T(8,128)(2,1)S(1)} %get-tuple-element.16), channel_id=1, source_target_pairs={{0,1},{1,0},{2,3},{3,2},{4,5},{5,4},{6,7},{7,6},{8,9},{9,8},{10,11... | collective-permute-start | bytes 1572872 | tf_op jit(solution)/shard_map/ppermute | solution.py:313
  36.0 5.0 %collective-permute-start.8 = (bf16[256,256]{1,0:T(8,128)(2,1)S(1)}, bf16[256,256]{1,0:T(8,128)(2,1)S(1)}, u32[]{:S(2)}, u32[]{:S(2)}) collective-permute-start(bf16[256,256]{1,0:T(8,128)(2,1)S(1)} %add_convert_fusion.2), channel_id=1, source_target_pairs={{0,4},{2,6},{4,0},{6,2},{8,12},{10,14},{12,8},{14,10},{1,5},{3,7},... | collective-permute-start | bytes 393224 | tf_op jit(solution)/shard_map/ppermute | solution.py:391
  36.0 11.1 %collective-permute-start.4 = (bf16[2,256,512]{2,1,0:T(8,128)(2,1)S(1)}, bf16[2,256,512]{2,1,0:T(8,128)(2,1)S(1)}, u32[]{:S(2)}, u32[]{:S(2)}) collective-permute-start(bf16[2,256,512]{2,1,0:T(8,128)(2,1)S(1)} %get-tuple-element.14), channel_id=1, source_target_pairs={{0,1},{1,0},{2,3},{3,2},{4,5},{5,4},{6,7},{7,6},{8,9},{9,8},{10,11... | collective-permute-start | bytes 1572872 | tf_op jit(solution)/shard_map/ppermute | solution.py:313
  41.0 6.0 %collective-permute-start.9 = (bf16[256,256]{1,0:T(8,128)(2,1)S(1)}, bf16[256,256]{1,0:T(8,128)(2,1)S(1)}, u32[]{:S(2)}, u32[]{:S(2)}) collective-permute-start(bf16[256,256]{1,0:T(8,128)(2,1)S(1)} %add_convert_fusion.1), channel_id=1, source_target_pairs={{0,8},{2,10},{4,12},{6,14},{8,0},{10,2},{12,4},{14,6},{1,9},{3,11}... | collective-permute-start | bytes 393224 | tf_op jit(solution)/shard_map/ppermute | solution.py:391
  41.4 17.8 %collective-permute-start.6 = (bf16[2,256,512]{2,1,0:T(8,128)(2,1)S(1)}, bf16[2,256,512]{2,1,0:T(8,128)(2,1)S(1)}, u32[]{:S(2)}, u32[]{:S(2)}) collective-permute-start(bf16[2,256,512]{2,1,0:T(8,128)(2,1)S(1)} %add_convert_fusion), channel_id=1, source_target_pairs={{0,2},{2,4},{4,6},{6,8},{8,10},{10,12},{12,14},{1,3},{3,5},{5,7},{... | collective-permute-start | bytes 1572872 | tf_op jit(solution)/shard_map/ppermute | solution.py:318
  47.1 1.6 %collective-permute-start.10 = (f32[256,256]{1,0:T(8,128)S(1)}, f32[256,256]{1,0:T(8,128)S(1)}, u32[]{:S(2)}, u32[]{:S(2)}) collective-permute-start(f32[256,256]{1,0:T(8,128)S(1)} %get-tuple-element.19), channel_id=1, source_target_pairs={{0,1},{1,0},{2,3},{3,2},{4,5},{5,4},{6,7},{7,6},{8,9},{9,8},{10,11... | collective-permute-start | bytes 786440 | tf_op jit(solution)/shard_map/ppermute | solution.py:313
